TPU v7x, 32 devices: a whole 2x2x4 slice. The times are simulated.
32 devices in a mesh: scene: 4 (over x, core), tile: 8 (over z, y).
Axes of the slice: x: 2, y: 2, z: 4, core: 2. Of those that a mesh axis runs over, the one named last changes fastest.
Arguments:
- image: bfloat16 [4, 8, 24, 32, 768], P('scene', 'tile'), may hold values from -6 to 6
- kernel: float32 [7, 7, 768], replicated, may hold values from -0.875 to 0.875
- ln_gain: float32 [768], replicated, may hold values from 0.5 to 2
- w_in: bfloat16 [768, 3072], replicated, may hold values from -0.21875 to 0.21875
- bias_in: float32 [3072], replicated, may hold values from -3 to 3
- w_out: bfloat16 [3072, 768], replicated, may hold values from -0.109375 to 0.109375
- layer_scale: float32 [768], replicated, may hold values from 0.5 to 2
- grad_rows: bfloat16 [26624, 768], P(('scene', 'tile')), may hold values from -6 to 6
- return_pos: int32 [26624], P(('scene', 'tile')), may hold values from 0 to 24575, as said below
- send_counts: int32 [32, 32], P(('scene', 'tile')), may hold values from 0 to 48, as said below
- send_offsets: int32 [32, 32], P(('scene', 'tile')), may hold values from 0 to 832, as said below
Outputs:
- grad_input: bfloat16 [4, 8, 24, 32, 768], P('scene', 'tile')
- grad_w_in: float32 [768, 3072], P(('scene', 'tile'))
- grad_w_out: float32 [3072, 768], P(('scene', 'tile'))
- grad_kernel: float32 [7, 7, 768], replicated
Inputs may be any that keep to these rules, and one draw needn't show every extreme that they name: `return_pos`: every row, live or not, lies in the segment d of its owner with the largest send_offsets[o, d] <= r, and names a position of device d's tile (between d * 768 and (d + 1) * 768 - 1); positions may repeat. `send_counts`: each owner has 768 live rows in all, at most 48 for one device, and exactly 48 for at least one device. For each owner, send_offsets[o, 0] = 0 and send_offsets[o, d + 1] - send_offsets[o, d] - send_counts[o, d] is 0, 1 or 2.
All inputs are finite; a program needn't handle non-finite values.
Results may differ from a plain program's by a relative error of at most 0.0064.
Values may be sent and summed in bfloat16 or wider, within the bound.
A program may use at most 128 MiB of HBM per device.

v0:
```python
import math

import jax
import jax.numpy as jnp
from jax import lax
from jax.sharding import PartitionSpec as P

KS = 7
GRID_W = 4


EPSILON = 1e-06
SQRT_TWO_PI = 0.7978845608028654
CUBIC = 0.044715


def passed_along(value, axis, steps):
    count = lax.axis_size(axis)
    leading, last = (max(0, -steps), min(count, count - steps))
    return lax.ppermute(value, axis, [(source, source + steps) for source in range(leading, last)])


def depthwise(padded, kernel, height, breadth):
    result = jnp.zeros((height, breadth, padded.shape[2]), jnp.float32)
    for k_row in range(KS):
        for k_col in range(KS):
            result = (
                result
                + kernel[k_row, k_col] * padded[k_row : k_row + height, k_col : k_col + breadth]
            )
    return result


def kernel_terms(upstream, padded, height, breadth):
    return jnp.stack(
        [
            jnp.stack(
                [
                    jnp.sum(
                        upstream * padded[k_row : k_row + height, k_col : k_col + breadth],
                        axis=(0, 1),
                    )
                    for k_col in range(KS)
                ]
            )
            for k_row in range(KS)
        ]
    )


def gelu_pair(hidden):
    inner_arg = SQRT_TWO_PI * (hidden + CUBIC * hidden * hidden * hidden)
    tangent = jnp.tanh(inner_arg)
    activated = 0.5 * hidden * (1.0 + tangent)
    derivative = 0.5 * (1.0 + tangent) + 0.5 * hidden * (1.0 - tangent * tangent) * SQRT_TWO_PI * (
        1.0 + 3.0 * CUBIC * hidden * hidden
    )
    return (activated, derivative)


def rim_shift(piece, offset_by, forward_pass):
    if forward_pass:
        return passed_along(piece, "tile", offset_by)
    return passed_along(piece, "tile", offset_by)


def rim_rows(tile_block, step_row, halo_width):
    if step_row == -1:
        return tile_block[tile_block.shape[0] - halo_width :]
    if step_row == 1:
        return tile_block[:halo_width]
    return tile_block


def rim_cols(tile_block, step_col, halo_width):
    if step_col == -1:
        return tile_block[:, tile_block.shape[1] - halo_width :]
    if step_col == 1:
        return tile_block[:, :halo_width]
    return tile_block


def extend(tile_block, forward_pass):
    halo_width = KS // 2
    grid_height = lax.axis_size("tile") // GRID_W
    tile_index = lax.axis_index("tile")
    grid_row = tile_index // GRID_W
    grid_col = tile_index % GRID_W
    row_bands = []
    for step_row in (-1, 0, 1):
        band_parts = []
        for step_col in (-1, 0, 1):
            if step_row == 0 and step_col == 0:
                band_parts.append(tile_block)
            else:
                piece = rim_cols(rim_rows(tile_block, step_row, halo_width), step_col, halo_width)
                present = (
                    (grid_row + step_row >= 0)
                    & (grid_row + step_row < grid_height)
                    & (grid_col + step_col >= 0)
                    & (grid_col + step_col < GRID_W)
                )
                received = rim_shift(piece, -(step_row * GRID_W + step_col), forward_pass)
                band_parts.append(jnp.where(present, received, jnp.zeros_like(received)))
        row_bands.append(jnp.concatenate(band_parts, axis=1))
    return jnp.concatenate(row_bands, axis=0)


def contract_rows(left_side, right_side):
    return lax.dot_general(
        left_side, right_side, (((0,), (0,)), ((), ())), preferred_element_type=jnp.float32
    )


def on_device(
    image,
    kernel,
    ln_gain,
    w_in,
    bias_in,
    w_out,
    layer_scale,
    grad_rows,
    return_pos,
    send_counts,
    send_offsets,
):
    scene_count = lax.axis_size("scene")
    tile_count = lax.axis_size("tile")
    peer_count = scene_count * tile_count
    height = image.shape[2]
    breadth = image.shape[3]
    channels = image.shape[4]
    tile_rows = height * breadth
    capacity = max(2, 2 * tile_rows // peer_count)
    slot_index = jnp.arange(capacity, dtype=jnp.int32)
    starts = send_offsets[0]
    counts = send_counts[0]
    filled = slot_index[None, :] < counts[:, None]
    picked = jnp.minimum(starts[:, None] + slot_index[None, :], grad_rows.shape[0] - 1)
    outgoing = jnp.where(filled[:, :, None], grad_rows[picked], jnp.zeros((), jnp.bfloat16))
    targets = jnp.where(filled, return_pos[picked] % tile_rows, -1)
    arrived, places = (
        lax.all_to_all(outgoing, ("scene", "tile"), split_axis=0, concat_axis=0, tiled=True),
        lax.all_to_all(targets, ("scene", "tile"), split_axis=0, concat_axis=0, tiled=True),
    )
    arrived = arrived.reshape(-1, channels)
    places = places.reshape(-1)
    own_block = image[0, 0]
    padded = extend(own_block, True).astype(jnp.float32)
    mixed_sum = depthwise(padded, kernel, height, breadth).reshape(tile_rows, channels)
    centre = mixed_sum - jnp.mean(mixed_sum, axis=-1, keepdims=True)
    inv_std = lax.rsqrt(jnp.mean(centre * centre, axis=-1, keepdims=True) + EPSILON)
    normed = centre * inv_std
    scaled = (normed * ln_gain).astype(jnp.bfloat16)
    hidden = jnp.dot(scaled, w_in, preferred_element_type=jnp.float32) + bias_in
    activated, derivative = gelu_pair(hidden)
    act_low = activated.astype(jnp.bfloat16)
    selector = (jnp.arange(tile_rows, dtype=jnp.int32)[:, None] == places[None, :]).astype(
        jnp.bfloat16
    )
    upstream = jnp.dot(selector, arrived, preferred_element_type=jnp.float32)
    branch_grad = (upstream * layer_scale).astype(jnp.bfloat16)
    act_grad = jnp.dot(branch_grad, w_out.T, preferred_element_type=jnp.float32)
    hidden_grad = (act_grad * derivative).astype(jnp.bfloat16)
    normed_grad = jnp.dot(hidden_grad, w_in.T, preferred_element_type=jnp.float32) * ln_gain
    mixed_grad = inv_std * (
        normed_grad
        - jnp.mean(normed_grad, axis=-1, keepdims=True)
        - normed * jnp.mean(normed_grad * normed, axis=-1, keepdims=True)
    )
    mixed_low = mixed_grad.astype(jnp.bfloat16).reshape(height, breadth, channels)
    grad_padded = extend(mixed_low, False).astype(jnp.float32)
    through = depthwise(grad_padded, kernel[::-1, ::-1], height, breadth)
    grad_input = (upstream.reshape(height, breadth, channels) + through).astype(jnp.bfloat16)
    factor = 1.0 / math.sqrt(tile_rows * peer_count)
    kernel_factor = 1.0 / math.sqrt(GRID_W * GRID_W * tile_rows)
    term_in = contract_rows(scaled, hidden_grad)
    term_out = contract_rows(act_low, branch_grad)
    first_in, first_out = (
        lax.psum_scatter(term_in, "scene", scatter_dimension=0, tiled=True),
        lax.psum_scatter(term_out, "scene", scatter_dimension=0, tiled=True),
    )
    grad_in, grad_out = (
        lax.psum_scatter(first_in, "tile", scatter_dimension=0, tiled=True),
        lax.psum_scatter(first_out, "tile", scatter_dimension=0, tiled=True),
    )
    local_kernel = kernel_terms(mixed_low.astype(jnp.float32), padded, height, breadth)
    grad_kernel = lax.psum(local_kernel, ("scene", "tile"))
    return (
        grad_input.reshape(image.shape),
        grad_in * factor,
        grad_out * factor,
        grad_kernel * kernel_factor,
    )


def solution(mesh):
    placed = (
        P("scene", "tile", None, None, None),
        P(),
        P(),
        P(),
        P(),
        P(),
        P(),
        P(("scene", "tile"), None),
        P(("scene", "tile")),
        P(("scene", "tile"), None),
        P(("scene", "tile"), None),
    )
    return jax.shard_map(
        on_device,
        mesh=mesh,
        in_specs=placed,
        out_specs=(
            P("scene", "tile", None, None, None),
            P(("scene", "tile"), None),
            P(("scene", "tile"), None),
            P(),
        ),
        check_vma=False,
    )
```

profile of v0, /device:TPU:0, one launch (start us, length us, event | category | flops | bytes accessed | tf_op | source)
XLA Modules:
  0.0 499.3 jit_solution(1575010512270566854)
XLA Ops:
  8.0 1.1 slice_bitcast_fusion.1
  9.1 1.3 collective-permute-start.6
  10.4 1.2 fusion.118
  11.6 1.3 collective-permute-start.4
  12.9 5.5 %collective-permute-start.3 = (bf16[24,3,768]{2,1,0:T(4,128)(2,1)S(1)}, bf16[24,3,768]{2,1,0:T(4,128)(2,1)S(1)}, u32[]{:S(2)}, u32[]{:S(2)}) collective-permute-start(bf16[24,3,768]{2,1,0:T(4,128)(2,1)S(1)} %get-tuple-element.112), channel_id=1, source_target_pairs={{0,1},{1,2},{2,3},{3,4},{4,5},{5,6},{6,7},{8,9},{9,10},{10,11},{11... | collective-permute-start | bytes 331784 | tf_op jit(solution)/shard_map/ppermute | solution.py:20
  18.4 5.5 %collective-permute-start.1 = (bf16[3,32,768]{2,1,0:T(8,128)(2,1)S(1)}, bf16[3,32,768]{2,1,0:T(8,128)(2,1)S(1)}, u32[]{:S(2)}, u32[]{:S(2)}) collective-permute-start(bf16[3,32,768]{2,1,0:T(8,128)(2,1)S(1)} %get-tuple-element.110), channel_id=1, source_target_pairs={{0,4},{1,5},{2,6},{3,7},{8,12},{9,13},{10,14},{11,15},{16,20},{17,... | collective-permute-start | bytes 442376 | tf_op jit(solution)/shard_map/ppermute | solution.py:20
  23.9 1.3 collective-permute-start.7
  25.2 0.7 compare_select_fusion.1
  26.1 5.9 %gather_fusion = s32[1536]{0:T(1024)S(1)} fusion(s32[832]{0:T(1024)S(1)} %copy-done.2, s32[2048]{0:T(1024)S(1)} %pad_clamp_fusion), kind=kCustom, calls=%fused_computation | custom fusion | bytes 18432 | tf_op jit(solution)/shard_map/gather | solution.py:142
  32.0 0.7 compare_select_fusion
  32.8 8.1 %all-to-all-start = ((s32[32,1,48]{2,1,0:T(1,128)}), s32[32,1,48]{2,1,0:T(1,128)S(1)}, u32[]{:S(2)}, u32[]{:S(2)}) async-start(s32[32,1,48]{2,1,0:T(1,128)} %compare_select_fusion), calls=%async_computation | async-start | bytes 32768 | tf_op jit(solution)/shard_map/all_to_all | solution.py:145
  40.9 0.2 slice_reduce_fusion.48
  41.0 0.2 slice_reduce_fusion.47
  41.3 5.7 %gather_fusion.1 = bf16[1536,768]{1,0:T(8,128)(2,1)} fusion(bf16[832,768]{1,0:T(8,128)(2,1)S(1)} %copy-done, s32[2048]{0:T(1024)S(1)} %pad_clamp_fusion), kind=kCustom, calls=%fused_computation.1 | custom fusion | bytes 4724736 | tf_op jit(solution)/shard_map/gather | solution.py:141
  47.0 3.4 broadcast_select_fusion
  50.3 0.1 slice_reduce_fusion.46
  50.5 6.0 %all-to-all-start.1 = ((bf16[32,48,768]{2,1,0:T(8,128)(2,1)}), bf16[32,48,768]{2,1,0:T(8,128)(2,1)}, u32[]{:S(2)}, u32[]{:S(2)}) async-start(bf16[32,48,768]{2,1,0:T(8,128)(2,1)} %broadcast_select_fusion), calls=%async_computation.1 | async-start | bytes 4718592 | tf_op jit(solution)/shard_map/all_to_all | solution.py:144
  56.5 0.5 broadcast.288
  57.0 0.7 reduce.103
  57.8 1.3 collective-permute-start.5
  59.1 23.7 %collective-permute-done.5 = bf16[3,3,768]{2,1,0:T(4,128)(2,1)S(1)} collective-permute-done((bf16[3,3,768]{2,1,0:T(4,128)(2,1)S(1)}, bf16[3,3,768]{2,1,0:T(4,128)(2,1)S(1)}, u32[]{:S(2)}, u32[]{:S(2)}) %collective-permute-start.5) | collective-permute-done | bytes 13856 | tf_op jit(solution)/shard_map/ppermute | solution.py:20
  82.9 20.3 %collective-permute-start.2 = (bf16[3,3,768]{2,1,0:T(4,128)(2,1)S(1)}, bf16[3,3,768]{2,1,0:T(4,128)(2,1)S(1)}, u32[]{:S(2)}, u32[]{:S(2)}) collective-permute-start(bf16[3,3,768]{2,1,0:T(4,128)(2,1)S(1)} %get-tuple-element.119), channel_id=1, source_target_pairs={{0,3},{1,4},{2,5},{3,6},{4,7},{8,11},{9,12},{10,13},{11,14},{12,15... | collective-permute-start | bytes 41480 | tf_op jit(solution)/shard_map/ppermute | solution.py:20
  103.2 1.4 collective-permute-done.2
  104.6 15.6 %collective-permute-start = (bf16[3,3,768]{2,1,0:T(4,128)(2,1)S(1)}, bf16[3,3,768]{2,1,0:T(4,128)(2,1)S(1)}, u32[]{:S(2)}, u32[]{:S(2)}) collective-permute-start(bf16[3,3,768]{2,1,0:T(4,128)(2,1)S(1)} %get-tuple-element.118), channel_id=1, source_target_pairs={{0,5},{1,6},{2,7},{8,13},{9,14},{10,15},{16,21},{17,22},{18,23},{2... | collective-permute-start | bytes 41480 | tf_op jit(solution)/shard_map/ppermute | solution.py:20
  120.2 1.4 collective-permute-done
  121.9 1.1 maximum_convert_fusion
  123.0 24.9 %fusion.115 = (f32[24,32]{1,0:T(8,128)S(1)}, f32[24,32,768]{2,1,0:T(8,128)}) fusion(f32[30,38,768]{2,1,0:T(8,128)S(1)} %maximum_convert_fusion, f32[768]{0:T(1024)S(1)} %get-tuple-element.55, f32[768]{0:T(1024)S(1)} %get-tuple-element.102, f32[768]{0:T(1024)S(1)} %get-tuple-element.103, f32[768]{0:T(1024)S(1)} %get-tuple-element.56, ...), kind=kLoop, calls=%fused_computation.317 | loop fusion | flops 57801984 | bytes 118118400 | tf_op jit(solution)/shard_map/reduce_sum | solution.py:152
  148.1 2.0 multiply_reduce_fusion.1
  150.2 2.0 multiply_convert_fusion.3
  152.2 8.5 %fusion.123 = f32[768,3072]{1,0:T(8,128)} fusion(bf16[768,768]{1,0:T(8,128)(2,1)S(1)} %multiply_convert_fusion.3, bf16[768,3072]{1,0:T(8,128)(2,1)} %param.14), kind=kOutput, calls=%fused_computation.325 | convolution fusion | flops 3623878656 | bytes 15335424 | tf_op jit(solution)/shard_map/dot_general | solution.py:156
  160.8 4.0 fusion.8
  164.8 0.4 copy-done.15
  165.2 11.1 %fusion.6 = bf16[768,3072]{1,0:T(8,128)(2,1)S(1)} fusion(f32[768,3072]{1,0:T(8,128)S(1)} %copy-done.15, bf16[3072,768]{1,0:T(8,128)(2,1)} %param.16, f32[3072]{0:T(1024)S(1)} %copy-done.13, f32[768,768]{1,0:T(8,128)S(1)} %fusion.8, f32[768]{0:T(1024)S(1)} %copy-done.14), kind=kOutput, calls=%fused_computation.59 | convolution fusion | flops 3672244224 | bytes 21249024 | tf_op jit(solution)/shard_map/dot_general | solution.py:164
  176.3 2.1 copy-done.6
  178.4 6.6 %fusion.124 = f32[768,3072]{1,0:T(8,128)} fusion(bf16[768,768]{1,0:T(8,128)(2,1)S(1)} %multiply_convert_fusion.3, bf16[768,3072]{1,0:T(8,128)(2,1)S(1)} %fusion.6), kind=kOutput, calls=%fused_computation.326 | convolution fusion | flops 3623878656 | bytes 15335424 | tf_op jit(solution)/shard_map/dot_general | solution.py:110
  185.1 8.7 %multiply_reduce_fusion.2 = (f32[768]{0:T(1024)S(1)}, f32[768]{0:T(1024)S(1)}, f32[768,768]{1,0:T(8,128)S(1)}) fusion(f32[768]{0:T(1024)S(1)} %copy-done.11, f32[768]{0:T(1024)S(1)} %rsqrt.12, f32[768]{0:T(1024)S(1)} %div.28, f32[24,32,768]{2,1,0:T(8,128)} %get-tuple-element.105, bf16[768,3072]{1,0:T(8,128)(2,1)} %copy-done.6, bf16[768,3072]{1,0:T(8,128)(2,1)} %param.14), kind=kOutput, calls=%fused_computation.222 | convolution fusion | flops 3627416064 | bytes 14171136 | tf_op jit(solution)/shard_map/dot_general | solution.py:166
  193.9 0.9 multiply_convert_fusion.2
  194.8 2.1 copy-done.4
  196.9 5.8 %fusion.56 = (f32[768]{0:T(1024)S(1)}, f32[768]{0:T(1024)S(1)}, f32[768]{0:T(1024)S(1)}, f32[768]{0:T(1024)S(1)}, f32[768]{0:T(1024)S(1)}, /*index=5*/f32[768]{0...) fusion(bf16[24,32,768]{2,1,0:T(8,128)(2,1)S(1)} %bitcast.49, ...), kind=kLoop, calls=%fused_computation.111 | loop fusion | flops 21809664 | bytes 43702272 | tf_op jit(solution)/shard_map/reduce_sum | solution.py:39
  202.6 5.7 %fusion.57 = (f32[768]{0:T(1024)S(1)}, f32[768]{0:T(1024)S(1)}, f32[768]{0:T(1024)S(1)}, f32[768]{0:T(1024)S(1)}, f32[768]{0:T(1024)S(1)}, /*index=5*/f32[768]{0...) fusion(bf16[24,32,768]{2,1,0:T(8,128)(2,1)S(1)} %bitcast.50, ...), kind=kLoop, calls=%fused_computation.112 | loop fusion | flops 21809664 | bytes 43702272 | tf_op jit(solution)/shard_map/reduce_sum | solution.py:39
  208.4 3.8 fusion.55
  213.2 0.7 copy-done.9
  213.8 0.3 reduce-scatter.9.cloned.1.call-start
  214.1 14.2 %fusion.7 = f32[3072,768]{1,0:T(8,128)} fusion(f32[768,3072]{1,0:T(8,128)} %fusion.123, f32[3072]{0:T(1024)S(1)} %copy-done.13, f32[768,768]{1,0:T(8,128)} %copy-done.8, f32[768]{0:T(1024)S(1)} %copy-done.14), kind=kOutput, calls=%fused_computation.62 | convolution fusion | flops 3648651264 | bytes 21249024 | tf_op jit(solution)/shard_map/dot_general | solution.py:110
  228.4 36.2 %reduce-scatter.5.cloned.1.call-done = f32[192,3072]{1,0:T(8,128)} async-done(((f32[768,3072]{1,0:T(8,128)}), f32[192,3072]{1,0:T(8,128)}) %reduce-scatter.5.cloned.1.call-update) | async-done | bytes 2359312 | tf_op jit(solution)/shard_map/reduce_scatter | solution.py:181
  264.6 4.3 collective-permute-start.9
  269.0 1.3 collective-permute-start.14
  270.3 1.3 collective-permute-start.13
  271.6 0.1 fusion.117
  271.7 1.3 collective-permute-start.12
  273.0 4.6 collective-permute-start.11
  277.6 6.3 %collective-permute-start.10 = (bf16[3,3,768]{2,1,0:T(4,128)(2,1)S(1)}, bf16[3,3,768]{2,1,0:T(4,128)(2,1)S(1)}, u32[]{:S(2)}, u32[]{:S(2)}) collective-permute-start(bf16[3,3,768]{2,1,0:T(4,128)(2,1)S(1)} %get-tuple-element.115), channel_id=1, source_target_pairs={{0,3},{1,4},{2,5},{3,6},{4,7},{8,11},{9,12},{10,13},{11,14},{12,15... | collective-permute-start | bytes 41480 | tf_op jit(solution)/shard_map/ppermute | solution.py:20
  284.0 1.4 collective-permute-done.10
  285.4 6.0 %collective-permute-start.8 = (bf16[3,3,768]{2,1,0:T(4,128)(2,1)S(1)}, bf16[3,3,768]{2,1,0:T(4,128)(2,1)S(1)}, u32[]{:S(2)}, u32[]{:S(2)}) collective-permute-start(bf16[3,3,768]{2,1,0:T(4,128)(2,1)S(1)} %get-tuple-element.114), channel_id=1, source_target_pairs={{0,5},{1,6},{2,7},{8,13},{9,14},{10,15},{16,21},{17,22},{18,23},{2... | collective-permute-start | bytes 41480 | tf_op jit(solution)/shard_map/ppermute | solution.py:20
  291.5 1.4 collective-permute-done.8
  292.9 1.3 collective-permute-start.15
  294.2 6.1 %collective-permute-done.15 = bf16[3,3,768]{2,1,0:T(4,128)(2,1)S(1)} collective-permute-done((bf16[3,3,768]{2,1,0:T(4,128)(2,1)S(1)}, bf16[3,3,768]{2,1,0:T(4,128)(2,1)S(1)}, u32[]{:S(2)}, u32[]{:S(2)}) %collective-permute-start.15) | collective-permute-done | bytes 13856 | tf_op jit(solution)/shard_map/ppermute | solution.py:20
  300.4 97.2 %all-reduce.2.cloned.1.call-done = f32[7,7,768]{2,1,0:T(8,128)} async-done(((f32[7,7,768]{2,1,0:T(8,128)}), f32[7,7,768]{2,1,0:T(8,128)}) %all-reduce.2.cloned.1.call-update) | async-done | bytes 150544 | tf_op jit(solution)/shard_map/psum | solution.py:189
  397.5 1.6 broadcast_multiply_fusion.2
  399.4 2.4 maximum_convert_fusion.1
  401.8 74.5 %fusion.110 = bf16[1,1,24,32,768]{4,3,2,1,0:T(8,128)(2,1)} fusion(f32[24,32,768]{2,1,0:T(8,128)} %bitcast.57, f32[30,38,768]{2,1,0:T(8,128)} %maximum_convert_fusion.1, f32[768]{0:T(1024)S(1)} %get-tuple-element.74, f32[768]{0:T(1024)S(1)} %get-tuple-element.93, f32[768]{0:T(1024)S(1)} %get-tuple-element.101, f32[768]{0:T(1024)S(1)} %get-tuple-element.100, ...), kind=kLoop, calls=%fused_computation.225 | loop fusion | flops 58392576 | bytes 119294976 | tf_op jit(solution)/shard_map/reshape | solution.py:191
  476.3 1.7 broadcast_multiply_fusion.1
  478.0 12.0 %reduce-scatter.11.cloned.1.call-done = f32[96,768]{1,0:T(8,128)} async-done(((f32[768,768]{1,0:T(8,128)}), f32[96,768]{1,0:T(8,128)}) %reduce-scatter.11.cloned.1.call-update) | async-done | bytes 294928 | tf_op jit(solution)/shard_map/reduce_scatter | solution.py:186
  490.0 1.7 broadcast_multiply_fusion
  (146 shorter events, 2.0 us)
Async XLA Ops:
  8.0 33.3 %copy-start = (bf16[832,768]{1,0:T(8,128)(2,1)S(1)}, bf16[832,768]{1,0:T(8,128)(2,1)}, u32[]{:S(2)}) copy-start(bf16[832,768]{1,0:T(8,128)(2,1)} %param.18) | copy-start | bytes 3833860
  8.0 18.0 %copy-start.2 = (s32[832]{0:T(1024)S(1)}, s32[832]{0:T(1024)}, u32[]{:S(2)}) copy-start(s32[832]{0:T(1024)} %param.19) | copy-start | bytes 9988
  9.1 112.7 %collective-permute-start.6 = (bf16[3,32,768]{2,1,0:T(8,128)(2,1)S(1)}, bf16[3,32,768]{2,1,0:T(8,128)(2,1)S(1)}, u32[]{:S(2)}, u32[]{:S(2)}) collective-permute-start(bf16[3,32,768]{2,1,0:T(8,128)(2,1)S(1)} %get-tuple-element.111), channel_id=1, source_target_pairs={{4,0},{5,1},{6,2},{7,3},{12,8},{13,9},{14,10},{15,11},{20,16},{21,... | collective-permute-start | bytes 442376 | tf_op jit(solution)/shard_map/ppermute | solution.py:20
  11.6 110.0 %collective-permute-start.4 = (bf16[24,3,768]{2,1,0:T(4,128)(2,1)S(1)}, bf16[24,3,768]{2,1,0:T(4,128)(2,1)S(1)}, u32[]{:S(2)}, u32[]{:S(2)}) collective-permute-start(bf16[24,3,768]{2,1,0:T(4,128)(2,1)S(1)} %get-tuple-element.113), channel_id=1, source_target_pairs={{1,0},{2,1},{3,2},{4,3},{5,4},{6,5},{7,6},{9,8},{10,9},{11,10},{12... | collective-permute-start | bytes 331784 | tf_op jit(solution)/shard_map/ppermute | solution.py:20
  12.9 108.8 %collective-permute-start.3 = (bf16[24,3,768]{2,1,0:T(4,128)(2,1)S(1)}, bf16[24,3,768]{2,1,0:T(4,128)(2,1)S(1)}, u32[]{:S(2)}, u32[]{:S(2)}) collective-permute-start(bf16[24,3,768]{2,1,0:T(4,128)(2,1)S(1)} %get-tuple-element.112), channel_id=1, source_target_pairs={{0,1},{1,2},{2,3},{3,4},{4,5},{5,6},{6,7},{8,9},{9,10},{10,11},{11... | collective-permute-start | bytes 331784 | tf_op jit(solution)/shard_map/ppermute | solution.py:20
  18.4 103.4 %collective-permute-start.1 = (bf16[3,32,768]{2,1,0:T(8,128)(2,1)S(1)}, bf16[3,32,768]{2,1,0:T(8,128)(2,1)S(1)}, u32[]{:S(2)}, u32[]{:S(2)}) collective-permute-start(bf16[3,32,768]{2,1,0:T(8,128)(2,1)S(1)} %get-tuple-element.110), channel_id=1, source_target_pairs={{0,4},{1,5},{2,6},{3,7},{8,12},{9,13},{10,14},{11,15},{16,20},{17,... | collective-permute-start | bytes 442376 | tf_op jit(solution)/shard_map/ppermute | solution.py:20
  23.9 33.9 %collective-permute-start.7 = (bf16[3,3,768]{2,1,0:T(4,128)(2,1)S(1)}, bf16[3,3,768]{2,1,0:T(4,128)(2,1)S(1)}, u32[]{:S(2)}, u32[]{:S(2)}) collective-permute-start(bf16[3,3,768]{2,1,0:T(4,128)(2,1)S(1)} %get-tuple-element.121), channel_id=1, source_target_pairs={{5,0},{6,1},{7,2},{13,8},{14,9},{15,10},{21,16},{22,17},{23,18},{2... | collective-permute-start | bytes 41480 | tf_op jit(solution)/shard_map/ppermute | solution.py:20
  26.0 6.0 %copy-start.12 = (s32[1,32]{1,0:T(1,128)S(1)}, s32[1,32]{1,0:T(1,128)}, u32[]{:S(2)}) copy-start(s32[1,32]{1,0:T(1,128)} %param.20) | copy-start | bytes 388
  26.1 14.8 %copy-start.10 = (f32[7,7,768]{2,1,0:T(8,128)S(1)}, f32[7,7,768]{2,1,0:T(8,128)}, u32[]{:S(2)}) copy-start(f32[7,7,768]{2,1,0:T(8,128)} %param.12) | copy-start | bytes 451588
  32.8 17.7 %all-to-all-start = ((s32[32,1,48]{2,1,0:T(1,128)}), s32[32,1,48]{2,1,0:T(1,128)S(1)}, u32[]{:S(2)}, u32[]{:S(2)}) async-start(s32[32,1,48]{2,1,0:T(1,128)} %compare_select_fusion), calls=%async_computation | async-start | bytes 32768 | tf_op jit(solution)/shard_map/all_to_all | solution.py:145
  50.5 71.4 %copy-start.7 = (bf16[1,1,24,32,768]{4,3,2,1,0:T(8,128)(2,1)S(1)}, bf16[1,1,24,32,768]{4,3,2,1,0:T(8,128)(2,1)}, u32[]{:S(2)}) copy-start(bf16[1,1,24,32,768]{4,3,2,1,0:T(8,128)(2,1)} %param.11) | copy-start | bytes 3538948
  50.5 110.2 %all-to-all-start.1 = ((bf16[32,48,768]{2,1,0:T(8,128)(2,1)}), bf16[32,48,768]{2,1,0:T(8,128)(2,1)}, u32[]{:S(2)}, u32[]{:S(2)}) async-start(bf16[32,48,768]{2,1,0:T(8,128)(2,1)} %broadcast_select_fusion), calls=%async_computation.1 | async-start | bytes 4718592 | tf_op jit(solution)/shard_map/all_to_all | solution.py:144
  56.5 208.1 %reduce-scatter.5.cloned.1.call-start = ((), (), s32[]{:S(2)}) async-start(), calls=%async_computation.6 | async-start | bytes 11796480 | tf_op jit(solution)/shard_map/reduce_scatter | solution.py:181
  57.8 25.1 %collective-permute-start.5 = (bf16[3,3,768]{2,1,0:T(4,128)(2,1)S(1)}, bf16[3,3,768]{2,1,0:T(4,128)(2,1)S(1)}, u32[]{:S(2)}, u32[]{:S(2)}) collective-permute-start(bf16[3,3,768]{2,1,0:T(4,128)(2,1)S(1)} %get-tuple-element.120), channel_id=1, source_target_pairs={{3,0},{4,1},{5,2},{6,3},{7,4},{11,8},{12,9},{13,10},{14,11},{15,12... | collective-permute-start | bytes 41480 | tf_op jit(solution)/shard_map/ppermute | solution.py:20
  82.9 21.8 %collective-permute-start.2 = (bf16[3,3,768]{2,1,0:T(4,128)(2,1)S(1)}, bf16[3,3,768]{2,1,0:T(4,128)(2,1)S(1)}, u32[]{:S(2)}, u32[]{:S(2)}) collective-permute-start(bf16[3,3,768]{2,1,0:T(4,128)(2,1)S(1)} %get-tuple-element.119), channel_id=1, source_target_pairs={{0,3},{1,4},{2,5},{3,6},{4,7},{8,11},{9,12},{10,13},{11,14},{12,15... | collective-permute-start | bytes 41480 | tf_op jit(solution)/shard_map/ppermute | solution.py:20
  104.6 17.0 %collective-permute-start = (bf16[3,3,768]{2,1,0:T(4,128)(2,1)S(1)}, bf16[3,3,768]{2,1,0:T(4,128)(2,1)S(1)}, u32[]{:S(2)}, u32[]{:S(2)}) collective-permute-start(bf16[3,3,768]{2,1,0:T(4,128)(2,1)S(1)} %get-tuple-element.118), channel_id=1, source_target_pairs={{0,5},{1,6},{2,7},{8,13},{9,14},{10,15},{16,21},{17,22},{18,23},{2... | collective-permute-start | bytes 41480 | tf_op jit(solution)/shard_map/ppermute | solution.py:20
  123.0 24.9 %copy-start.3 = (f32[30,38,768]{2,1,0:T(8,128)}, f32[30,38,768]{2,1,0:T(8,128)S(1)}, u32[]{:S(2)}) copy-start(f32[30,38,768]{2,1,0:T(8,128)S(1)} %maximum_convert_fusion) | copy-start | bytes 10506244
  148.0 2.2 copy-start.11
  160.7 4.0 copy-start.13
  160.7 4.0 copy-start.14
  160.7 4.4 copy-start.15
  165.2 11.1 %copy-start.8 = (f32[768,768]{1,0:T(8,128)}, f32[768,768]{1,0:T(8,128)S(1)}, u32[]{:S(2)}) copy-start(f32[768,768]{1,0:T(8,128)S(1)} %fusion.8) | copy-start | bytes 7077892
  176.3 2.2 copy-start.6
  185.0 212.5 %all-reduce.2.cloned.1.call-start = ((), (), s32[]{:S(2)}) async-start(), calls=%async_computation.10 | async-start | bytes 344064 | tf_op jit(solution)/shard_map/psum | solution.py:189
  185.1 8.8 %copy-start.5 = (f32[24,32,768]{2,1,0:T(8,128)S(1)}, f32[24,32,768]{2,1,0:T(8,128)}, u32[]{:S(2)}) copy-start(f32[24,32,768]{2,1,0:T(8,128)} %get-tuple-element.105) | copy-start | bytes 7077892
  193.9 3.0 copy-start.4
  213.1 0.7 copy-start.9
  213.8 187.9 %reduce-scatter.9.cloned.1.call-start = ((), (), s32[]{:S(2)}) async-start(), calls=%async_computation.8 | async-start | bytes 11796480 | tf_op jit(solution)/shard_map/reduce_scatter | solution.py:182
  228.3 248.0 %reduce-scatter.7.cloned.1.call-start = ((), (), s32[]{:S(2)}) async-start(), calls=%async_computation.7 | async-start | bytes 2654208 | tf_op jit(solution)/shard_map/reduce_scatter | solution.py:185
  264.5 225.5 %reduce-scatter.11.cloned.1.call-start = ((), (), s32[]{:S(2)}) async-start(), calls=%async_computation.9 | async-start | bytes 2654208 | tf_op jit(solution)/shard_map/reduce_scatter | solution.py:186
  264.6 134.7 %collective-permute-start.9 = (bf16[3,32,768]{2,1,0:T(8,128)(2,1)S(1)}, bf16[3,32,768]{2,1,0:T(8,128)(2,1)S(1)}, u32[]{:S(2)}, u32[]{:S(2)}) collective-permute-start(bf16[3,32,768]{2,1,0:T(8,128)(2,1)S(1)} %bitcast.60), channel_id=1, source_target_pairs={{0,4},{1,5},{2,6},{3,7},{8,12},{9,13},{10,14},{11,15},{16,20},{17,... | collective-permute-start | bytes 442376 | tf_op jit(solution)/shard_map/ppermute | solution.py:20
  269.0 130.4 %collective-permute-start.14 = (bf16[3,32,768]{2,1,0:T(8,128)(2,1)S(1)}, bf16[3,32,768]{2,1,0:T(8,128)(2,1)S(1)}, u32[]{:S(2)}, u32[]{:S(2)}) collective-permute-start(bf16[3,32,768]{2,1,0:T(8,128)(2,1)S(1)} %bitcast.58), channel_id=1, source_target_pairs={{4,0},{5,1},{6,2},{7,3},{12,8},{13,9},{14,10},{15,11},{20,16},{21,... | collective-permute-start | bytes 442376 | tf_op jit(solution)/shard_map/ppermute | solution.py:20
  270.3 7.3 %collective-permute-start.13 = (bf16[3,3,768]{2,1,0:T(4,128)(2,1)S(1)}, bf16[3,3,768]{2,1,0:T(4,128)(2,1)S(1)}, u32[]{:S(2)}, u32[]{:S(2)}) collective-permute-start(bf16[3,3,768]{2,1,0:T(4,128)(2,1)S(1)} %get-tuple-element.116), channel_id=1, source_target_pairs={{3,0},{4,1},{5,2},{6,3},{7,4},{11,8},{12,9},{13,10},{14,11},{15,12... | collective-permute-start | bytes 41480 | tf_op jit(solution)/shard_map/ppermute | solution.py:20
  271.7 127.4 %collective-permute-start.12 = (bf16[24,3,768]{2,1,0:T(4,128)(2,1)S(1)}, bf16[24,3,768]{2,1,0:T(4,128)(2,1)S(1)}, u32[]{:S(2)}, u32[]{:S(2)}) collective-permute-start(bf16[24,3,768]{2,1,0:T(4,128)(2,1)S(1)} %get-tuple-element.109), channel_id=1, source_target_pairs={{1,0},{2,1},{3,2},{4,3},{5,4},{6,5},{7,6},{9,8},{10,9},{11,10},{12... | collective-permute-start | bytes 331784 | tf_op jit(solution)/shard_map/ppermute | solution.py:20
  273.0 126.2 %collective-permute-start.11 = (bf16[24,3,768]{2,1,0:T(4,128)(2,1)S(1)}, bf16[24,3,768]{2,1,0:T(4,128)(2,1)S(1)}, u32[]{:S(2)}, u32[]{:S(2)}) collective-permute-start(bf16[24,3,768]{2,1,0:T(4,128)(2,1)S(1)} %get-tuple-element.108), channel_id=1, source_target_pairs={{0,1},{1,2},{2,3},{3,4},{4,5},{5,6},{6,7},{8,9},{9,10},{10,11},{11... | collective-permute-start | bytes 331784 | tf_op jit(solution)/shard_map/ppermute | solution.py:20
  277.6 7.8 %collective-permute-start.10 = (bf16[3,3,768]{2,1,0:T(4,128)(2,1)S(1)}, bf16[3,3,768]{2,1,0:T(4,128)(2,1)S(1)}, u32[]{:S(2)}, u32[]{:S(2)}) collective-permute-start(bf16[3,3,768]{2,1,0:T(4,128)(2,1)S(1)} %get-tuple-element.115), channel_id=1, source_target_pairs={{0,3},{1,4},{2,5},{3,6},{4,7},{8,11},{9,12},{10,13},{11,14},{12,15... | collective-permute-start | bytes 41480 | tf_op jit(solution)/shard_map/ppermute | solution.py:20
  285.4 7.5 %collective-permute-start.8 = (bf16[3,3,768]{2,1,0:T(4,128)(2,1)S(1)}, bf16[3,3,768]{2,1,0:T(4,128)(2,1)S(1)}, u32[]{:S(2)}, u32[]{:S(2)}) collective-permute-start(bf16[3,3,768]{2,1,0:T(4,128)(2,1)S(1)} %get-tuple-element.114), channel_id=1, source_target_pairs={{0,5},{1,6},{2,7},{8,13},{9,14},{10,15},{16,21},{17,22},{18,23},{2... | collective-permute-start | bytes 41480 | tf_op jit(solution)/shard_map/ppermute | solution.py:20
  292.9 7.4 %collective-permute-start.15 = (bf16[3,3,768]{2,1,0:T(4,128)(2,1)S(1)}, bf16[3,3,768]{2,1,0:T(4,128)(2,1)S(1)}, u32[]{:S(2)}, u32[]{:S(2)}) collective-permute-start(bf16[3,3,768]{2,1,0:T(4,128)(2,1)S(1)} %get-tuple-element.117), channel_id=1, source_target_pairs={{5,0},{6,1},{7,2},{13,8},{14,9},{15,10},{21,16},{22,17},{23,18},{2... | collective-permute-start | bytes 41480 | tf_op jit(solution)/shard_map/ppermute | solution.py:20
  401.8 90.0 %copy-start.1 = (bf16[832,768]{1,0:T(8,128)(2,1)S(1)}, bf16[832,768]{1,0:T(8,128)(2,1)}, u32[]{:S(2)}) copy-start(bf16[832,768]{1,0:T(8,128)(2,1)} %param.18) | copy-start | bytes 3833860
Sparse Core Ops, SparseCore 0:
  185.2 79.3 reduce-scatter.4
  267.1 78.7 reduce-scatter.8
  349.4 69.2 reduce-scatter.6
  422.0 68.0 reduce-scatter.10
Sparse Core Ops, SparseCore 1:
  213.9 183.6 all-reduce.1
where the time goes:
time: 503 us; the launch traced here: 499 us
  waiting for transfers between devices  181 us (36%)
  other arithmetic  134 us (27%)
  starting transfers between devices  92.9 us (18%)
  matrix products  53.1 us (11%)
  local copies, waits for them, and re-layouts  21.3 us (4%)
  between operations  16.9 us (3%)
    psum x1, waiting for transfers between devices, on_device(): grad_kernel = lax.psum(local_kernel, ('scene', 'tile'))  97.2 us
    ppermute x16, starting transfers between devices, passed_along(): lax.ppermute(value, axis, [(source, source + steps) for source in range(l...  78.4 us
    reshape x1, other arithmetic, on_device(): grad_input.reshape(image.shape)  74.5 us
    reduce_scatter x1, waiting for transfers between devices, on_device(): lax.psum_scatter(term_in, 'scene', scatter_dimension=0, tiled=True)  36.2 us
    ppermute x16, waiting for transfers between devices, passed_along(): lax.ppermute(value, axis, [(source, source + steps) for source in range(l...  35.6 us
    reduce_sum x1, other arithmetic, on_device(): centre = mixed_sum - jnp.mean(mixed_sum, axis=-1, keepdims=True)  24.9 us
    dot_general x2, matrix products, contract_rows(): lax.dot_general(left_side, right_side, (((0,), (0,)), ((), ())), preferre...  20.8 us
    reduce_sum x3, other arithmetic, kernel_terms(): jnp.sum(upstream * padded[k_row:k_row + height, k_col:k_col + breadth], a...  15.2 us
  transfers between devices with their start and end apart: 23, of which 9 were waited for; matrix products, arithmetic and copies ran while one was open for 36% of the time, Pallas kernels for 0%

commit v1 on v0

v1 whole, which is shorter than its diff:
```python
import math

import jax
import jax.numpy as jnp
from jax import lax
from jax.experimental import pallas as pl
from jax.experimental.pallas import tpu as pltpu
from jax.sharding import PartitionSpec as P

KS = 7
GRID_W = 4


EPSILON = 1e-06
SQRT_TWO_PI = 0.7978845608028654
CUBIC = 0.044715


LANES = 128
GROUP = 4


def widen(padded_ref, wide_ref):
    rows, cols = padded_ref.shape[0], padded_ref.shape[1]

    @pl.loop(0, rows)
    def _(row):
        wide_ref[row, pl.ds(0, cols), :] = padded_ref[row].astype(jnp.float32)


def conv_rows(wide_ref, kernel_ref, first, breadth, flip):
    sums = [jnp.zeros((breadth, LANES), jnp.float32) for _ in range(GROUP)]
    for col in range(KS):
        for row in range(GROUP + KS - 1):
            piece = wide_ref[first + row, pl.ds(col, breadth), :]
            for out in range(GROUP):
                tap = row - out
                if 0 <= tap < KS:
                    k_row, k_col = (KS - 1 - tap, KS - 1 - col) if flip else (tap, col)
                    sums[out] = sums[out] + kernel_ref[k_row, pl.ds(k_col, 1), :] * piece
    return sums


def forward_body(padded_ref, kernel_ref, out_ref, wide_ref):
    height, breadth = out_ref.shape[0], out_ref.shape[1]
    widen(padded_ref, wide_ref)

    @pl.loop(0, height // GROUP)
    def _(group):
        first = group * GROUP
        sums = conv_rows(wide_ref, kernel_ref, first, breadth, False)
        for out in range(GROUP):
            out_ref[first + out] = sums[out]


def backward_body(padded_ref, kernel_ref, up_ref, out_ref, wide_ref):
    height, breadth = out_ref.shape[0], out_ref.shape[1]
    widen(padded_ref, wide_ref)

    @pl.loop(0, height // GROUP)
    def _(group):
        first = group * GROUP
        sums = conv_rows(wide_ref, kernel_ref, first, breadth, True)
        for out in range(GROUP):
            out_ref[first + out] = (sums[out] + up_ref[first + out]).astype(out_ref.dtype)


def terms_body(grad_ref, padded_ref, out_ref, wide_ref):
    height, breadth = grad_ref.shape[0], grad_ref.shape[1]
    widen(padded_ref, wide_ref)
    for col in range(KS):

        def step(group, sums):
            first = group * GROUP
            sums = list(sums)
            grads = [grad_ref[first + out].astype(jnp.float32) for out in range(GROUP)]
            for row in range(GROUP + KS - 1):
                piece = wide_ref[first + row, pl.ds(col, breadth), :]
                for out in range(GROUP):
                    tap = row - out
                    if 0 <= tap < KS:
                        prod = (grads[out] * piece).reshape(breadth // 8, 8, LANES)
                        sums[tap] = sums[tap] + jnp.sum(prod, axis=0)
            return tuple(sums)

        zeros = tuple(jnp.zeros((8, LANES), jnp.float32) for _ in range(KS))
        sums = lax.fori_loop(0, height // GROUP, step, zeros)
        for tap in range(KS):
            out_ref[tap, pl.ds(col, 1), :] = jnp.sum(sums[tap], axis=0, keepdims=True)


def by_lanes(shape):
    return pl.BlockSpec(tuple(shape[:2]) + (LANES,), lambda lane: (0, 0, lane))


def lane_call(body, args, out_shape, out_type, wide):
    flops = 2 * KS * KS * wide[0] * wide[1] * out_shape[2]
    return pl.pallas_call(
        body,
        out_shape=jax.ShapeDtypeStruct(out_shape, out_type),
        grid=(out_shape[2] // LANES,),
        in_specs=[by_lanes(arg.shape) for arg in args],
        out_specs=by_lanes(out_shape),
        scratch_shapes=[pltpu.VMEM((wide[0], -(-wide[1] // 8) * 8, LANES), jnp.float32)],
        compiler_params=pltpu.CompilerParams(vmem_limit_bytes=24 * 2**20),
        cost_estimate=pl.CostEstimate(flops=flops * 100, bytes_accessed=40 * 2**20, transcendentals=0),
    )(*args)


def extend(block):
    halo = KS // 2
    tiles = lax.axis_size("tile")
    right_pairs = [(t, t + 1) for t in range(tiles) if t % GRID_W < GRID_W - 1]
    left_pairs = [(b, a) for a, b in right_pairs]
    down_pairs = [(t, t + GRID_W) for t in range(tiles - GRID_W)]
    up_pairs = [(b, a) for a, b in down_pairs]
    left = lax.ppermute(block[:, -halo:], "tile", right_pairs)
    right = lax.ppermute(block[:, :halo], "tile", left_pairs)
    wide = jnp.concatenate([left, block, right], axis=1)
    top = lax.ppermute(wide[-halo:], "tile", down_pairs)
    bottom = lax.ppermute(wide[:halo], "tile", up_pairs)
    return jnp.concatenate([top, wide, bottom], axis=0)


def summed(value):
    for axis in ("scene", "tile"):
        count = lax.axis_size(axis)
        bit = 1
        while bit < count:
            value = value + lax.ppermute(value, axis, [(d, d ^ bit) for d in range(count)])
            bit *= 2
    return value


def gelu_pair(hidden):
    inner_arg = SQRT_TWO_PI * (hidden + CUBIC * hidden * hidden * hidden)
    tangent = jnp.tanh(inner_arg)
    activated = 0.5 * hidden * (1.0 + tangent)
    derivative = 0.5 * (1.0 + tangent) + 0.5 * hidden * (1.0 - tangent * tangent) * SQRT_TWO_PI * (
        1.0 + 3.0 * CUBIC * hidden * hidden
    )
    return (activated, derivative)


def contract_rows(left_side, right_side):
    return lax.dot_general(
        left_side, right_side, (((0,), (0,)), ((), ())), preferred_element_type=jnp.float32
    )


def on_device(
    image,
    kernel,
    ln_gain,
    w_in,
    bias_in,
    w_out,
    layer_scale,
    grad_rows,
    return_pos,
    send_counts,
    send_offsets,
):
    scene_count = lax.axis_size("scene")
    tile_count = lax.axis_size("tile")
    peer_count = scene_count * tile_count
    height = image.shape[2]
    breadth = image.shape[3]
    channels = image.shape[4]
    tile_rows = height * breadth
    capacity = max(2, 2 * tile_rows // peer_count)
    starts = send_offsets[0]
    counts = send_counts[0]
    slot_index = jnp.arange(capacity, dtype=jnp.int32)
    filled = (slot_index[None, :] < counts[:, None]).reshape(-1)
    picked = (starts[:, None] + slot_index[None, :]).reshape(-1)
    own_slots = jnp.arange(grad_rows.shape[0], dtype=jnp.int32)
    chosen = (picked[:, None] == own_slots[None, :]) & filled[:, None]
    outgoing = jnp.dot(
        chosen.astype(jnp.bfloat16), grad_rows, preferred_element_type=jnp.float32
    ).astype(jnp.bfloat16)
    local_places = return_pos % tile_rows + 1
    targets = jnp.sum(jnp.where(chosen, local_places[None, :], 0), axis=1) - 1
    own_block = image[0, 0]
    padded = extend(own_block)
    outgoing, targets, padded = lax.optimization_barrier((outgoing, targets, padded))
    arrived, places = (
        lax.all_to_all(
            outgoing.reshape(peer_count, capacity, channels),
            ("scene", "tile"), split_axis=0, concat_axis=0, tiled=True,
        ),
        lax.all_to_all(
            targets.reshape(peer_count, capacity),
            ("scene", "tile"), split_axis=0, concat_axis=0, tiled=True,
        ),
    )
    arrived = arrived.reshape(-1, channels)
    places = places.reshape(-1)
    mixed_sum = lane_call(
        forward_body, (padded, kernel), (height, breadth, channels), jnp.float32, padded.shape
    ).reshape(tile_rows, channels)
    centre = mixed_sum - jnp.mean(mixed_sum, axis=-1, keepdims=True)
    inv_std = lax.rsqrt(jnp.mean(centre * centre, axis=-1, keepdims=True) + EPSILON)
    normed = centre * inv_std
    scaled = (normed * ln_gain).astype(jnp.bfloat16)
    hidden = jnp.dot(scaled, w_in, preferred_element_type=jnp.float32) + bias_in
    activated, derivative = gelu_pair(hidden)
    act_low = activated.astype(jnp.bfloat16)
    selector = (jnp.arange(tile_rows, dtype=jnp.int32)[:, None] == places[None, :]).astype(
        jnp.bfloat16
    )
    upstream = jnp.dot(selector, arrived, preferred_element_type=jnp.float32)
    branch_grad = (upstream * layer_scale).astype(jnp.bfloat16)
    act_grad = jnp.dot(branch_grad, w_out.T, preferred_element_type=jnp.float32)
    hidden_grad = (act_grad * derivative).astype(jnp.bfloat16)
    normed_grad = jnp.dot(hidden_grad, w_in.T, preferred_element_type=jnp.float32) * ln_gain
    mixed_grad = inv_std * (
        normed_grad
        - jnp.mean(normed_grad, axis=-1, keepdims=True)
        - normed * jnp.mean(normed_grad * normed, axis=-1, keepdims=True)
    )
    mixed_low = mixed_grad.astype(jnp.bfloat16).reshape(height, breadth, channels)
    grad_padded = extend(mixed_low)
    grad_input = lane_call(
        backward_body,
        (grad_padded, kernel, upstream.reshape(height, breadth, channels)),
        (height, breadth, channels),
        jnp.bfloat16,
        grad_padded.shape,
    )
    factor = 1.0 / math.sqrt(tile_rows * peer_count)
    kernel_factor = 1.0 / math.sqrt(GRID_W * GRID_W * tile_rows)
    term_out = contract_rows(act_low, branch_grad).astype(jnp.bfloat16)
    term_in = contract_rows(scaled, hidden_grad).astype(jnp.bfloat16)
    first_out, first_in = (
        lax.psum_scatter(term_out, "scene", scatter_dimension=0, tiled=True),
        lax.psum_scatter(term_in, "scene", scatter_dimension=0, tiled=True),
    )
    grad_out, grad_in = (
        lax.psum_scatter(first_out, "tile", scatter_dimension=0, tiled=True).astype(jnp.float32),
        lax.psum_scatter(first_in, "tile", scatter_dimension=0, tiled=True).astype(jnp.float32),
    )
    local_kernel = lane_call(
        terms_body, (mixed_low, padded), (KS, KS, channels), jnp.float32, padded.shape
    )
    grad_kernel = summed(local_kernel)
    return (
        grad_input.reshape(image.shape),
        grad_in * factor,
        grad_out * factor,
        grad_kernel * kernel_factor,
    )


def solution(mesh):
    placed = (
        P("scene", "tile", None, None, None),
        P(),
        P(),
        P(),
        P(),
        P(),
        P(),
        P(("scene", "tile"), None),
        P(("scene", "tile")),
        P(("scene", "tile"), None),
        P(("scene", "tile"), None),
    )
    return jax.shard_map(
        on_device,
        mesh=mesh,
        in_specs=placed,
        out_specs=(
            P("scene", "tile", None, None, None),
            P(("scene", "tile"), None),
            P(("scene", "tile"), None),
            P(),
        ),
        check_vma=False,
    )
```

time: 503 us -> 381 us (0.76)
  other arithmetic: 134 us -> 16.8 us
  starting transfers between devices: 92.9 us -> 34.1 us
  Pallas kernels: 0 us -> 39 us
  waiting for transfers between devices: 181 us -> 202 us
  local copies, waits for them, and re-layouts: 21.3 us -> 7.16 us
  blocking collectives: 0 us -> 10.6 us
    psum x1 -> x0, waiting for transfers between devices: 97.2 us -> none  [on_device(): grad_kernel = lax.psum(local_kernel, ('scene', 'tile'))]
    reshape x1 -> x0, other arithmetic: 74.5 us -> none  [on_device(): grad_input.reshape(image.shape)]
    reduce_scatter x1, waiting for transfers between devices: 12 us -> 64.7 us  [on_device(): lax.psum_scatter(first_out, 'tile', scatter_dimension=0, tiled=True)]
    ppermute x16 -> x13, starting transfers between devices: 78.4 us -> 29.8 us  [the longest x2 8.82 us: extend(): top = lax.ppermute(wide[-halo:], 'tile', down_pairs)]
    pallas_call x0 -> x3, Pallas kernels: none -> 39 us  [lane_call(): pl.pallas_call(body, out_shape=jax.ShapeDtypeStruct(out_shape, out_type),...]
    reduce_scatter x1, waiting for transfers between devices: 0.01 us -> 28.8 us  [on_device(): lax.psum_scatter(term_out, 'scene', scatter_dimension=0, tiled=True)]
    reduce_scatter x1, waiting for transfers between devices: 0.02 us -> 25.5 us  [on_device(): lax.psum_scatter(first_in, 'tile', scatter_dimension=0, tiled=True)]
    all_to_all x2 -> x1, waiting for transfers between devices: 0.01 us -> 24.1 us  [on_device(): lax.all_to_all(outgoing.reshape(peer_count, capacity, channels), ('scene'...]
  transfers between devices with their start and end apart: 23 -> 18, of which waited for: 9 -> 12; matrix products, arithmetic and copies ran while one was open for 36% -> 13% of each run, Pallas kernels for 0% -> 10%
where the time goes in v1:
time: 381 us; the launch traced here: 380 us
  waiting for transfers between devices  202 us (53%)
  matrix products  55.9 us (15%)
  Pallas kernels  39 us (10%)
  starting transfers between devices  34.1 us (9%)
  other arithmetic  16.8 us (4%)
  between operations  14.2 us (4%)
  blocking collectives  10.6 us (3%)
  local copies, waits for them, and re-layouts  7.16 us (2%)
    reduce_scatter x1, waiting for transfers between devices, on_device(): lax.psum_scatter(first_out, 'tile', scatter_dimension=0, tiled=True)  64.7 us
    pallas_call x3, Pallas kernels, lane_call(): pl.pallas_call(body, out_shape=jax.ShapeDtypeStruct(out_shape, out_type),...  39 us
    reduce_scatter x1, waiting for transfers between devices, on_device(): lax.psum_scatter(term_in, 'scene', scatter_dimension=0, tiled=True)  32.2 us
    reduce_scatter x1, waiting for transfers between devices, on_device(): lax.psum_scatter(term_out, 'scene', scatter_dimension=0, tiled=True)  28.8 us
    reduce_scatter x1, waiting for transfers between devices, on_device(): lax.psum_scatter(first_in, 'tile', scatter_dimension=0, tiled=True)  25.5 us
    all_to_all x1, waiting for transfers between devices, on_device(): lax.all_to_all(outgoing.reshape(peer_count, capacity, channels), ('scene'...  24.1 us
    dot_general x2, matrix products, contract_rows(): lax.dot_general(left_side, right_side, (((0,), (0,)), ((), ())), preferre...  18.9 us
    ppermute x2, waiting for transfers between devices, extend(): bottom = lax.ppermute(wide[:halo], 'tile', up_pairs)  15 us
  transfers between devices with their start and end apart: 18, of which 12 were waited for; matrix products, arithmetic and copies ran while one was open for 13% of the time, Pallas kernels for 10%

profile of v1, /device:TPU:0, one launch (start us, length us, event | category | flops | bytes accessed | tf_op | source)
XLA Modules:
  0.0 380.0 jit_solution(11035159462177630857)
XLA Ops:
  7.2 1.3 fusion.24
  8.5 4.9 %collective-permute-start = (bf16[24,3,768]{2,1,0:T(4,128)(2,1)S(1)}, bf16[24,3,768]{2,1,0:T(4,128)(2,1)S(1)}, u32[]{:S(2)}, u32[]{:S(2)}) collective-permute-start(bf16[24,3,768]{2,1,0:T(4,128)(2,1)S(1)} %get-tuple-element.18), channel_id=1, source_target_pairs={{0,1},{1,2},{2,3},{4,5},{5,6},{6,7},{8,9},{9,10},{10,11},{12,13},{... | collective-permute-start | bytes 331784 | tf_op jit(solution)/shard_map/ppermute | solution.py:117
  13.3 1.3 collective-permute-start.1
  14.6 0.7 iota_add_fusion
  15.4 0.1 add.97
  15.4 0.7 iota_compare_fusion.3
  16.2 0.1 lt.29
  16.3 0.7 fusion.18
  17.0 4.5 %fusion.11 = bf16[1536,768]{1,0:T(8,128)(2,1)} fusion(bf16[832,768]{1,0:T(8,128)(2,1)S(1)} %copy-done, s32[1536]{0:T(1024)S(1)} %add.97, pred[1536]{0:T(1024)(128)(4,1)S(1)} %lt.29), kind=kOutput, calls=%fused_computation.18 | convolution fusion | flops 1966669824 | bytes 3644928 | tf_op jit(solution)/shard_map/dot_general | solution.py:179
  21.5 1.1 select_reduce_fusion
  22.6 0.1 pad_maximum_fusion.7
  22.8 4.5 %collective-permute-start.2 = (bf16[3,38,768]{2,1,0:T(8,128)(2,1)S(1)}, bf16[3,38,768]{2,1,0:T(8,128)(2,1)S(1)}, u32[]{:S(2)}, u32[]{:S(2)}) collective-permute-start(bf16[3,38,768]{2,1,0:T(8,128)(2,1)S(1)} %get-tuple-element.14), channel_id=1, source_target_pairs={{0,4},{1,5},{2,6},{3,7},{8,12},{9,13},{10,14},{11,15},{16,20},{17,... | collective-permute-start | bytes 525320 | tf_op jit(solution)/shard_map/ppermute | solution.py:120
  27.3 1.3 collective-permute-start.3
  28.6 2.3 collective-permute-done.2
  30.9 8.9 %collective-permute-done.3 = bf16[3,38,768]{2,1,0:T(8,128)(2,1)S(1)} collective-permute-done((bf16[3,38,768]{2,1,0:T(8,128)(2,1)S(1)}, bf16[3,38,768]{2,1,0:T(8,128)(2,1)S(1)}, u32[]{:S(2)}, u32[]{:S(2)}) %collective-permute-start.3) | collective-permute-done | bytes 175136 | tf_op jit(solution)/shard_map/ppermute | solution.py:121
  39.8 0.8 pad_maximum_fusion.padded_ref
  40.7 0.1 all_to_all.9
  40.8 10.6 %all_to_all.14 = s32[32,1,48]{2,1,0:T(1,128)S(1)} all-to-all(s32[32,1,48]{2,1,0:T(1,128)S(1)} %all_to_all.9), channel_id=1, replica_groups=mesh['scene'=4,'tile'=8] {'scene','tile'}, dimensions={0} | all-to-all | bytes 12288 | tf_op jit(solution)/shard_map/all_to_all | solution.py:192
  51.4 3.6 all-to-all-start.1
  55.0 0.2 reduce-scatter.5.cloned.1.call-start
  55.3 13.9 %shard_map.138 = f32[24,32,768]{2,1,0:T(8,128)S(1)} custom-call(bf16[30,38,768]{2,1,0:T(8,128)(2,1)S(1)} %pad_maximum_fusion.padded_ref, f32[7,7,768]{2,1,0:T(8,128)S(1)} %copy-done.5), custom_call_target="tpu_custom_call" | custom-call | flops 8580096000 | bytes 41943040 | tf_op jit(solution)/shard_map/pallas_call | solution.py:98
  69.2 1.4 copy-done.1
  70.6 1.9 reduce_sum.46
  72.6 2.0 multiply_reduce_fusion.1
  74.7 2.0 multiply_convert_fusion.3
  76.7 8.7 %fusion.25 = f32[768,3072]{1,0:T(8,128)} fusion(bf16[768,768]{1,0:T(8,128)(2,1)S(1)} %multiply_convert_fusion.3, bf16[768,3072]{1,0:T(8,128)(2,1)} %param.14), kind=kOutput, calls=%fused_computation.56 | convolution fusion | flops 3623878656 | bytes 15335424 | tf_op jit(solution)/shard_map/dot_general | solution.py:206
  85.4 0.5 broadcast.91
  85.9 0.7 reduce.5
  86.7 24.1 %all-to-all-done.1 = bf16[32,48,768]{2,1,0:T(8,128)(2,1)} async-done(((bf16[32,48,768]{2,1,0:T(8,128)(2,1)}), bf16[32,48,768]{2,1,0:T(8,128)(2,1)}, u32[]{:S(2)}, u32[]{:S(2)}) %all-to-all-start.1) | async-done | bytes 2359328 | tf_op jit(solution)/shard_map/all_to_all | solution.py:188
  110.8 4.0 %fusion.10 = f32[768,768]{1,0:T(8,128)S(1)} fusion(bf16[1536,768]{1,0:T(8,128)(2,1)} %bitcast.4, s32[1536]{0:T(1024)S(1)} %eq.34), kind=kOutput, calls=%fused_computation.17 | convolution fusion | flops 1813118976 | bytes 4724736 | tf_op jit(solution)/shard_map/dot_general | solution.py:212
  114.8 0.4 copy-done.13
  115.3 11.1 %fusion.6 = bf16[768,3072]{1,0:T(8,128)(2,1)S(1)} fusion(f32[768,3072]{1,0:T(8,128)S(1)} %copy-done.13, bf16[3072,768]{1,0:T(8,128)(2,1)} %param.16, f32[3072]{0:T(1024)S(1)} %copy-done.10, f32[768,768]{1,0:T(8,128)S(1)} %fusion.10, f32[768]{0:T(1024)S(1)} %copy-done.11), kind=kOutput, calls=%fused_computation.8 | convolution fusion | flops 3672244224 | bytes 21249024 | tf_op jit(solution)/shard_map/dot_general | solution.py:214
  126.3 2.2 copy-done.12
  128.6 5.7 %convolution_convert_fusion.1 = bf16[768,3072]{1,0:T(8,128)(2,1)} fusion(bf16[768,768]{1,0:T(8,128)(2,1)S(1)} %multiply_convert_fusion.3, bf16[768,3072]{1,0:T(8,128)(2,1)S(1)} %fusion.6), kind=kOutput, calls=%fused_computation.15 | convolution fusion | flops 3626237952 | bytes 10616832 | tf_op jit(solution)/shard_map/dot_general | solution.py:146
  134.3 0.3 reduce-scatter.9.cloned.1.call-start
  134.6 13.2 %convolution_convert_fusion = bf16[3072,768]{1,0:T(8,128)(2,1)} fusion(f32[768,3072]{1,0:T(8,128)} %fusion.25, f32[3072]{0:T(1024)S(1)} %copy-done.10, f32[768,768]{1,0:T(8,128)} %copy-done.6, f32[768]{0:T(1024)S(1)} %copy-done.11), kind=kOutput, calls=%fused_computation.14 | convolution fusion | flops 3651010560 | bytes 16530432 | tf_op jit(solution)/shard_map/dot_general | solution.py:146
  147.9 32.2 %reduce-scatter.5.cloned.1.call-done = bf16[192,3072]{1,0:T(8,128)(2,1)} async-done(((bf16[768,3072]{1,0:T(8,128)(2,1)}), bf16[192,3072]{1,0:T(8,128)(2,1)}) %reduce-scatter.5.cloned.1.call-update) | async-done | bytes 1179664 | tf_op jit(solution)/shard_map/reduce_scatter | solution.py:237
  180.1 8.7 %multiply_reduce_fusion.2 = (f32[768]{0:T(1024)S(1)}, f32[768]{0:T(1024)S(1)}, f32[768,768]{1,0:T(8,128)S(1)}) fusion(f32[768]{0:T(1024)S(1)} %copy-done.9, f32[768]{0:T(1024)S(1)} %rsqrt.12, f32[768]{0:T(1024)S(1)} %div.16, f32[24,32,768]{2,1,0:T(8,128)} %copy-done.1, bf16[768,3072]{1,0:T(8,128)(2,1)} %copy-done.12, bf16[768,3072]{1,0:T(8,128)(2,1)} %param.14), kind=kOutput, calls=%fused_computation.29 | convolution fusion | flops 3627416064 | bytes 14171136 | tf_op jit(solution)/shard_map/dot_general | solution.py:216
  188.9 0.9 multiply_convert_fusion.2
  189.8 0.6 copy-done.4
  190.4 11.4 %shard_map.140 = f32[7,7,768]{2,1,0:T(8,128)S(1)} custom-call(bf16[24,32,768]{2,1,0:T(8,128)(2,1)S(1)} %bitcast.27, bf16[30,38,768]{2,1,0:T(8,128)(2,1)S(1)} %copy-done.4), custom_call_target="tpu_custom_call" | custom-call | flops 8580096000 | bytes 41943040 | tf_op jit(solution)/shard_map/pallas_call | solution.py:98
  201.9 28.8 %reduce-scatter.9.cloned.1.call-done = bf16[768,768]{1,0:T(8,128)(2,1)} async-done(((bf16[3072,768]{1,0:T(8,128)(2,1)}), bf16[768,768]{1,0:T(8,128)(2,1)}) %reduce-scatter.9.cloned.1.call-update) | async-done | bytes 1179664 | tf_op jit(solution)/shard_map/reduce_scatter | solution.py:236
  230.7 0.1 fusion.23
  230.8 3.4 collective-permute-start.4
  234.2 1.3 collective-permute-start.5
  235.5 0.6 collective-permute-start.9
  236.1 1.1 collective-permute-done.4
  237.3 4.1 %collective-permute-done.5 = bf16[24,3,768]{2,1,0:T(4,128)(2,1)S(1)} collective-permute-done((bf16[24,3,768]{2,1,0:T(4,128)(2,1)S(1)}, bf16[24,3,768]{2,1,0:T(4,128)(2,1)S(1)}, u32[]{:S(2)}, u32[]{:S(2)}) %collective-permute-start.5) | collective-permute-done | bytes 110624 | tf_op jit(solution)/shard_map/ppermute | solution.py:118
  241.4 0.1 pad_maximum_fusion.4
  241.5 4.3 %collective-permute-start.6 = (bf16[3,38,768]{2,1,0:T(8,128)(2,1)S(1)}, bf16[3,38,768]{2,1,0:T(8,128)(2,1)S(1)}, u32[]{:S(2)}, u32[]{:S(2)}) collective-permute-start(bf16[3,38,768]{2,1,0:T(8,128)(2,1)S(1)} %get-tuple-element.12), channel_id=1, source_target_pairs={{0,4},{1,5},{2,6},{3,7},{8,12},{9,13},{10,14},{11,15},{16,20},{17,... | collective-permute-start | bytes 525320 | tf_op jit(solution)/shard_map/ppermute | solution.py:120
  245.8 1.3 collective-permute-start.7
  247.2 2.4 collective-permute-start.10
  249.6 3.6 collective-permute-done.10
  253.2 2.3 collective-permute-start.11
  255.6 6.1 %collective-permute-done.7 = bf16[3,38,768]{2,1,0:T(8,128)(2,1)S(1)} collective-permute-done((bf16[3,38,768]{2,1,0:T(8,128)(2,1)S(1)}, bf16[3,38,768]{2,1,0:T(8,128)(2,1)S(1)}, u32[]{:S(2)}, u32[]{:S(2)}) %collective-permute-start.7) | collective-permute-done | bytes 175136 | tf_op jit(solution)/shard_map/ppermute | solution.py:121
  261.7 0.9 pad_maximum_fusion.1.padded_ref
  262.5 0.9 collective-permute-done.11
  263.5 2.1 collective-permute-start.12
  265.6 13.7 %shard_map.139 = bf16[24,32,768]{2,1,0:T(8,128)(2,1)} custom-call(bf16[30,38,768]{2,1,0:T(8,128)(2,1)S(1)} %pad_maximum_fusion.1.padded_ref, f32[7,7,768]{2,1,0:T(8,128)S(1)} %copy-done.5, f32[24,32,768]{2,1,0:T(8,128)S(1)} %bitcast.31), custom_call_target="tpu_custom_call" | custom-call | flops 8580096000 | bytes 41943040 | tf_op jit(solution)/shard_map/pallas_call | solution.py:98
  279.3 0.7 add_multiply_fusion
  280.0 25.5 %reduce-scatter.7.cloned.1.call-done = bf16[24,3072]{1,0:T(8,128)(2,1)} async-done(((bf16[192,3072]{1,0:T(8,128)(2,1)}), bf16[24,3072]{1,0:T(8,128)(2,1)}) %reduce-scatter.7.cloned.1.call-update) | async-done | bytes 147472 | tf_op jit(solution)/shard_map/reduce_scatter | solution.py:241
  305.5 1.6 convert_multiply_fusion.1
  307.1 64.7 %reduce-scatter.11.cloned.1.call-done = bf16[96,768]{1,0:T(8,128)(2,1)} async-done(((bf16[768,768]{1,0:T(8,128)(2,1)}), bf16[96,768]{1,0:T(8,128)(2,1)}) %reduce-scatter.11.cloned.1.call-update) | async-done | bytes 147472 | tf_op jit(solution)/shard_map/reduce_scatter | solution.py:240
  371.8 1.6 convert_multiply_fusion
  (48 shorter events, 0.6 us)
Async XLA Ops:
  7.2 9.8 %copy-start = (bf16[832,768]{1,0:T(8,128)(2,1)S(1)}, bf16[832,768]{1,0:T(8,128)(2,1)}, u32[]{:S(2)}) copy-start(bf16[832,768]{1,0:T(8,128)(2,1)} %param.18) | copy-start | bytes 3833860
  8.5 14.1 %collective-permute-start = (bf16[24,3,768]{2,1,0:T(4,128)(2,1)S(1)}, bf16[24,3,768]{2,1,0:T(4,128)(2,1)S(1)}, u32[]{:S(2)}, u32[]{:S(2)}) collective-permute-start(bf16[24,3,768]{2,1,0:T(4,128)(2,1)S(1)} %get-tuple-element.18), channel_id=1, source_target_pairs={{0,1},{1,2},{2,3},{4,5},{5,6},{6,7},{8,9},{9,10},{10,11},{12,13},{... | collective-permute-start | bytes 331784 | tf_op jit(solution)/shard_map/ppermute | solution.py:117
  13.3 9.3 %collective-permute-start.1 = (bf16[24,3,768]{2,1,0:T(4,128)(2,1)S(1)}, bf16[24,3,768]{2,1,0:T(4,128)(2,1)S(1)}, u32[]{:S(2)}, u32[]{:S(2)}) collective-permute-start(bf16[24,3,768]{2,1,0:T(4,128)(2,1)S(1)} %get-tuple-element.19), channel_id=1, source_target_pairs={{1,0},{2,1},{3,2},{5,4},{6,5},{7,6},{9,8},{10,9},{11,10},{13,12},{... | collective-permute-start | bytes 331784 | tf_op jit(solution)/shard_map/ppermute | solution.py:118
  17.0 5.6 %copy-start.8 = (bf16[1,1,24,32,768]{4,3,2,1,0:T(8,128)(2,1)S(1)}, bf16[1,1,24,32,768]{4,3,2,1,0:T(8,128)(2,1)}, u32[]{:S(2)}) copy-start(bf16[1,1,24,32,768]{4,3,2,1,0:T(8,128)(2,1)} %param.11) | copy-start | bytes 3538948
  22.8 8.1 %collective-permute-start.2 = (bf16[3,38,768]{2,1,0:T(8,128)(2,1)S(1)}, bf16[3,38,768]{2,1,0:T(8,128)(2,1)S(1)}, u32[]{:S(2)}, u32[]{:S(2)}) collective-permute-start(bf16[3,38,768]{2,1,0:T(8,128)(2,1)S(1)} %get-tuple-element.14), channel_id=1, source_target_pairs={{0,4},{1,5},{2,6},{3,7},{8,12},{9,13},{10,14},{11,15},{16,20},{17,... | collective-permute-start | bytes 525320 | tf_op jit(solution)/shard_map/ppermute | solution.py:120
  27.3 12.6 %collective-permute-start.3 = (bf16[3,38,768]{2,1,0:T(8,128)(2,1)S(1)}, bf16[3,38,768]{2,1,0:T(8,128)(2,1)S(1)}, u32[]{:S(2)}, u32[]{:S(2)}) collective-permute-start(bf16[3,38,768]{2,1,0:T(8,128)(2,1)S(1)} %get-tuple-element.15), channel_id=1, source_target_pairs={{4,0},{5,1},{6,2},{7,3},{12,8},{13,9},{14,10},{15,11},{20,16},{21,... | collective-permute-start | bytes 525320 | tf_op jit(solution)/shard_map/ppermute | solution.py:121
  40.7 14.6 %copy-start.3 = (bf16[30,38,768]{2,1,0:T(8,128)(2,1)}, bf16[30,38,768]{2,1,0:T(8,128)(2,1)S(1)}, u32[]{:S(2)}) copy-start(bf16[30,38,768]{2,1,0:T(8,128)(2,1)S(1)} %pad_maximum_fusion.padded_ref) | copy-start | bytes 5253124
  51.4 3.9 %copy-start.5 = (f32[7,7,768]{2,1,0:T(8,128)S(1)}, f32[7,7,768]{2,1,0:T(8,128)}, u32[]{:S(2)}) copy-start(f32[7,7,768]{2,1,0:T(8,128)} %kernel_ref.3) | copy-start | bytes 451588
  51.4 59.5 %all-to-all-start.1 = ((bf16[32,48,768]{2,1,0:T(8,128)(2,1)}), bf16[32,48,768]{2,1,0:T(8,128)(2,1)}, u32[]{:S(2)}, u32[]{:S(2)}) async-start(bf16[32,48,768]{2,1,0:T(8,128)(2,1)} %bitcast.35), calls=%async_computation.1 | async-start | bytes 4718592 | tf_op jit(solution)/shard_map/all_to_all | solution.py:188
  55.0 125.0 %reduce-scatter.5.cloned.1.call-start = ((), (), s32[]{:S(2)}) async-start(), calls=%async_computation.6 | async-start | bytes 5898240 | tf_op jit(solution)/shard_map/reduce_scatter | solution.py:237
  69.2 1.5 copy-start.1
  70.6 4.1 %copy-start.9 = (f32[768]{0:T(1024)S(1)}, f32[768]{0:T(1024)}, u32[]{:S(2)}) copy-start(f32[768]{0:T(1024)} %param.13) | copy-start | bytes 9220
  110.8 4.0 %copy-start.10 = (f32[3072]{0:T(1024)S(1)}, f32[3072]{0:T(1024)}, u32[]{:S(2)}) copy-start(f32[3072]{0:T(1024)} %param.15) | copy-start | bytes 36868
  110.8 4.0 %copy-start.11 = (f32[768]{0:T(1024)S(1)}, f32[768]{0:T(1024)}, u32[]{:S(2)}) copy-start(f32[768]{0:T(1024)} %param.17) | copy-start | bytes 9220
  110.8 4.4 %copy-start.13 = (f32[768,3072]{1,0:T(8,128)S(1)}, f32[768,3072]{1,0:T(8,128)}, u32[]{:S(2)}) copy-start(f32[768,3072]{1,0:T(8,128)} %fusion.25) | copy-start | bytes 28311556
  115.3 11.1 %copy-start.6 = (f32[768,768]{1,0:T(8,128)}, f32[768,768]{1,0:T(8,128)S(1)}, u32[]{:S(2)}) copy-start(f32[768,768]{1,0:T(8,128)S(1)} %fusion.10) | copy-start | bytes 7077892
  126.3 2.2 copy-start.12
  134.3 96.3 %reduce-scatter.9.cloned.1.call-start = ((), (), s32[]{:S(2)}) async-start(), calls=%async_computation.8 | async-start | bytes 5898240 | tf_op jit(solution)/shard_map/reduce_scatter | solution.py:236
  147.8 157.6 %reduce-scatter.7.cloned.1.call-start = ((), (), s32[]{:S(2)}) async-start(), calls=%async_computation.7 | async-start | bytes 1327104 | tf_op jit(solution)/shard_map/reduce_scatter | solution.py:241
  180.1 191.7 %reduce-scatter.11.cloned.1.call-start = ((), (), s32[]{:S(2)}) async-start(), calls=%async_computation.9 | async-start | bytes 1327104 | tf_op jit(solution)/shard_map/reduce_scatter | solution.py:240
  180.1 8.8 %copy-start.2 = (f32[24,32,768]{2,1,0:T(8,128)S(1)}, f32[24,32,768]{2,1,0:T(8,128)}, u32[]{:S(2)}) copy-start(f32[24,32,768]{2,1,0:T(8,128)} %copy-done.1) | copy-start | bytes 7077892
  188.9 1.5 copy-start.4
  201.8 33.7 %collective-permute-start.8 = (f32[7,7,768]{2,1,0:T(8,128)S(1)}, f32[7,7,768]{2,1,0:T(8,128)S(1)}, u32[]{:S(2)}, u32[]{:S(2)}) collective-permute-start(f32[7,7,768]{2,1,0:T(8,128)S(1)} %shard_map.140), channel_id=1, source_target_pairs={{0,8},{8,0},{16,24},{24,16},{1,9},{9,1},{17,25},{25,17},{2,10},{10... | collective-permute-start | bytes 451592 | tf_op jit(solution)/shard_map/ppermute | solution.py:130
  230.8 6.5 %collective-permute-start.4 = (bf16[24,3,768]{2,1,0:T(4,128)(2,1)S(1)}, bf16[24,3,768]{2,1,0:T(4,128)(2,1)S(1)}, u32[]{:S(2)}, u32[]{:S(2)}) collective-permute-start(bf16[24,3,768]{2,1,0:T(4,128)(2,1)S(1)} %get-tuple-element.16), channel_id=1, source_target_pairs={{0,1},{1,2},{2,3},{4,5},{5,6},{6,7},{8,9},{9,10},{10,11},{12,13},{... | collective-permute-start | bytes 331784 | tf_op jit(solution)/shard_map/ppermute | solution.py:117
  234.2 7.2 %collective-permute-start.5 = (bf16[24,3,768]{2,1,0:T(4,128)(2,1)S(1)}, bf16[24,3,768]{2,1,0:T(4,128)(2,1)S(1)}, u32[]{:S(2)}, u32[]{:S(2)}) collective-permute-start(bf16[24,3,768]{2,1,0:T(4,128)(2,1)S(1)} %get-tuple-element.17), channel_id=1, source_target_pairs={{1,0},{2,1},{3,2},{5,4},{6,5},{7,6},{9,8},{10,9},{11,10},{13,12},{... | collective-permute-start | bytes 331784 | tf_op jit(solution)/shard_map/ppermute | solution.py:118
  235.5 11.6 %collective-permute-start.9 = (f32[7,7,768]{2,1,0:T(8,128)S(1)}, f32[7,7,768]{2,1,0:T(8,128)S(1)}, u32[]{:S(2)}, u32[]{:S(2)}) collective-permute-start(f32[7,7,768]{2,1,0:T(8,128)S(1)} %add.110), channel_id=1, source_target_pairs={{0,16},{8,24},{16,0},{24,8},{1,17},{9,25},{17,1},{25,9},{2,18},{10... | collective-permute-start | bytes 451592 | tf_op jit(solution)/shard_map/ppermute | solution.py:130
  241.5 14.1 %collective-permute-start.6 = (bf16[3,38,768]{2,1,0:T(8,128)(2,1)S(1)}, bf16[3,38,768]{2,1,0:T(8,128)(2,1)S(1)}, u32[]{:S(2)}, u32[]{:S(2)}) collective-permute-start(bf16[3,38,768]{2,1,0:T(8,128)(2,1)S(1)} %get-tuple-element.12), channel_id=1, source_target_pairs={{0,4},{1,5},{2,6},{3,7},{8,12},{9,13},{10,14},{11,15},{16,20},{17,... | collective-permute-start | bytes 525320 | tf_op jit(solution)/shard_map/ppermute | solution.py:120
  245.8 15.8 %collective-permute-start.7 = (bf16[3,38,768]{2,1,0:T(8,128)(2,1)S(1)}, bf16[3,38,768]{2,1,0:T(8,128)(2,1)S(1)}, u32[]{:S(2)}, u32[]{:S(2)}) collective-permute-start(bf16[3,38,768]{2,1,0:T(8,128)(2,1)S(1)} %get-tuple-element.13), channel_id=1, source_target_pairs={{4,0},{5,1},{6,2},{7,3},{12,8},{13,9},{14,10},{15,11},{20,16},{21,... | collective-permute-start | bytes 525320 | tf_op jit(solution)/shard_map/ppermute | solution.py:121
  247.2 18.4 %copy-start.7 = (f32[768,768]{1,0:T(8,128)S(1)}, f32[768,768]{1,0:T(8,128)}, u32[]{:S(2)}) copy-start(f32[768,768]{1,0:T(8,128)} %copy-done.6) | copy-start | bytes 7077892
  247.2 6.0 %collective-permute-start.10 = (f32[7,7,768]{2,1,0:T(8,128)S(1)}, f32[7,7,768]{2,1,0:T(8,128)S(1)}, u32[]{:S(2)}, u32[]{:S(2)}) collective-permute-start(f32[7,7,768]{2,1,0:T(8,128)S(1)} %add.111), channel_id=1, source_target_pairs={{0,1},{1,0},{2,3},{3,2},{4,5},{5,4},{6,7},{7,6},{8,9},{9,8},{10,11... | collective-permute-start | bytes 451592 | tf_op jit(solution)/shard_map/ppermute | solution.py:130
  253.2 10.2 %collective-permute-start.11 = (f32[7,7,768]{2,1,0:T(8,128)S(1)}, f32[7,7,768]{2,1,0:T(8,128)S(1)}, u32[]{:S(2)}, u32[]{:S(2)}) collective-permute-start(f32[7,7,768]{2,1,0:T(8,128)S(1)} %add.112), channel_id=1, source_target_pairs={{0,2},{1,3},{2,0},{3,1},{4,6},{5,7},{6,4},{7,5},{8,10},{9,11},{10,... | collective-permute-start | bytes 451592 | tf_op jit(solution)/shard_map/ppermute | solution.py:130
  263.5 15.8 %collective-permute-start.12 = (f32[7,7,768]{2,1,0:T(8,128)S(1)}, f32[7,7,768]{2,1,0:T(8,128)S(1)}, u32[]{:S(2)}, u32[]{:S(2)}) collective-permute-start(f32[7,7,768]{2,1,0:T(8,128)S(1)} %add.113), channel_id=1, source_target_pairs={{0,4},{1,5},{2,6},{3,7},{4,0},{5,1},{6,2},{7,3},{8,12},{9,13},{10,... | collective-permute-start | bytes 451592 | tf_op jit(solution)/shard_map/ppermute | solution.py:130
Sparse Core Ops, SparseCore 0:
  134.4 45.5 reduce-scatter.4
  182.7 47.8 reduce-scatter.8
  234.0 71.3 reduce-scatter.6
  308.7 63.0 reduce-scatter.10

commit v2 on v1

--- a/solution.py
+++ b/solution.py
@@ -1,3 +1,4 @@
+import functools
 import math
 
 import jax
@@ -122,14 +123,232 @@
     return jnp.concatenate([top, wide, bottom], axis=0)
 
 
-def summed(value):
-    for axis in ("scene", "tile"):
-        count = lax.axis_size(axis)
-        bit = 1
-        while bit < count:
-            value = value + lax.ppermute(value, axis, [(d, d ^ bit) for d in range(count)])
-            bit *= 2
-    return value
+MESH = pl.DeviceIdType.MESH
+SIDES = [(r, c) for r in (-1, 0, 1) for c in (-1, 0, 1) if (r, c) != (0, 0)]
+
+
+def bits_of(count):
+    return [1 << k for k in reversed(range(count.bit_length() - 1))]
+
+
+def place_of(scenes, tiles):
+    return [("scene", bit) for bit in bits_of(scenes)] + [("tile", bit) for bit in bits_of(tiles)]
+
+
+def exchange_body(
+    scenes, tiles, factor, kernel_factor,
+    in_ref, out_ref, grad_ref, first_ref, last_ref, local_ref,
+    w_in_ref, w_out_ref, kernel_ref, *rest,
+):
+    places = place_of(scenes, tiles)
+    steps = len(places)
+    halos = rest[:8]
+    rest = rest[8:]
+    got_in, got_out = rest[:steps], rest[steps : 2 * steps]
+    got_kernel, sent_kernel, send_sems, recv_sems, halo_send, halo_recv = rest[2 * steps :]
+    me = {"scene": lax.axis_index("scene"), "tile": lax.axis_index("tile")}
+    scene_bits = [p for p in places if p[0] == "scene"][::-1]
+    tile_bits = [p for p in places if p[0] == "tile"][::-1]
+    order_in = scene_bits + tile_bits
+    order_out = scene_bits[:1] + tile_bits + scene_bits[1:]
+
+    def half(place):
+        return lax.rem(me[place[0]] // place[1], 2)
+
+    def partner(place):
+        return {place[0]: me[place[0]] + place[1] * (1 - 2 * half(place))}
+
+    grid_row, grid_col = me["tile"] // GRID_W, lax.rem(me["tile"], GRID_W)
+
+    def present(side):
+        row, col = grid_row + side[0], grid_col + side[1]
+        return (row >= 0) & (row < tiles // GRID_W) & (col >= 0) & (col < GRID_W)
+
+    def neighbour(side):
+        return {"tile": me["tile"] + side[0] * GRID_W + side[1]}
+
+    barrier = pltpu.get_barrier_semaphore()
+    for place in places:
+        pl.semaphore_signal(barrier, inc=1, device_id=partner(place), device_id_type=MESH)
+    for side in SIDES:
+
+        @pl.when(present(side))
+        def _():
+            pl.semaphore_signal(barrier, inc=1, device_id=neighbour(side), device_id_type=MESH)
+
+    pl.semaphore_wait(
+        barrier, steps + sum(jnp.where(present(side), 1, 0).astype(jnp.int32) for side in SIDES)
+    )
+
+    def position(order, step):
+        left = [p for p in places if p not in order[:step]]
+        return left.index(order[step])
+
+    def weight_copy(which, order, source, got, step):
+        place = order[step]
+        pos = position(order, step)
+        src = source if step == 0 else got[step - 1]
+        return pltpu.make_async_remote_copy(
+            src_ref=src.at[(slice(None),) * pos + (1 - half(place),)],
+            dst_ref=got[step],
+            send_sem=send_sems.at[which, step],
+            recv_sem=recv_sems.at[which, step],
+            device_id=partner(place),
+            device_id_type=MESH,
+        )
+
+    def weight_add(order, source, got, step, result):
+        pos = position(order, step)
+        src = source if step == 0 else got[step - 1]
+        dims = steps - 1 - step
+        mine = half(order[step])
+
+        def one(chunk, carry):
+            index = tuple(lax.rem(chunk // (1 << (dims - 1 - d)), 2) for d in range(dims))
+            held = index[:pos] + (mine,) + index[pos:]
+            total = got[step][index].astype(jnp.float32) + src[held].astype(jnp.float32)
+            got[step][index] = total.astype(jnp.bfloat16)
+            return carry
+
+        if dims:
+            lax.fori_loop(0, 1 << dims, one, 0)
+        else:
+            total = got[step][...].astype(jnp.float32) + src[mine].astype(jnp.float32)
+            result[...] = total * factor
+
+    def kernel_copy(step):
+        return pltpu.make_async_remote_copy(
+            src_ref=sent_kernel.at[step],
+            dst_ref=got_kernel.at[step],
+            send_sem=send_sems.at[2, step],
+            recv_sem=recv_sems.at[2, step],
+            device_id=partner(order_in[step]),
+            device_id_type=MESH,
+        )
+
+    def halo_copy(number):
+        row, col = SIDES[number]
+        source = {-1: first_ref, 0: grad_ref, 1: last_ref}[col]
+        width = KS // 2
+        if row == -1:
+            source = source.at[pl.ds(0, width)]
+        elif row == 1:
+            source = source.at[pl.ds(grad_ref.shape[0] - width, width)]
+        return pltpu.make_async_remote_copy(
+            src_ref=source,
+            dst_ref=halos[SIDES.index((-row, -col))],
+            send_sem=halo_send.at[number],
+            recv_sem=halo_recv.at[SIDES.index((-row, -col))],
+            device_id=neighbour((row, col)),
+            device_id_type=MESH,
+        )
+
+    def halo_arrival(number):
+        row, col = SIDES[number]
+        return pltpu.make_async_remote_copy(
+            src_ref=halos[number],
+            dst_ref=halos[number],
+            send_sem=halo_send.at[number],
+            recv_sem=halo_recv.at[number],
+            device_id=neighbour((row, col)),
+            device_id_type=MESH,
+        )
+
+    for number in range(8):
+
+        @pl.when(present(SIDES[number]))
+        def _():
+            halo_copy(number).start()
+
+    copies_in = [weight_copy(0, order_in, in_ref, got_in, step) for step in range(steps)]
+    copies_out = [weight_copy(1, order_out, out_ref, got_out, step) for step in range(steps)]
+    copies_kernel = [kernel_copy(step) for step in range(steps)]
+    copies_in[0].start()
+    copies_out[0].start()
+    sent_kernel[0] = local_ref[...]
+    copies_kernel[0].start()
+    for step in range(steps):
+        later = step < steps - 1
+        copies_in[step].wait_recv()
+        weight_add(order_in, in_ref, got_in, step, w_in_ref)
+        if later:
+            copies_in[step + 1].start()
+        copies_out[step].wait_recv()
+        weight_add(order_out, out_ref, got_out, step, w_out_ref)
+        if later:
+            copies_out[step + 1].start()
+        copies_kernel[step].wait_recv()
+        if later:
+            sent_kernel[step + 1] = sent_kernel[step] + got_kernel[step]
+            copies_kernel[step + 1].start()
+        else:
+            kernel_ref[...] = (sent_kernel[step] + got_kernel[step]) * kernel_factor
+    for number in range(8):
+
+        @pl.when(present(SIDES[number]))
+        def _():
+            halo_copy(number).wait_send()
+            halo_arrival(number).wait_recv()
+
+        @pl.when(jnp.logical_not(present(SIDES[number])))
+        def _():
+            halos[number][...] = jnp.zeros(halos[number].shape, halos[number].dtype)
+
+    for step in range(steps):
+        copies_in[step].wait_send()
+        copies_out[step].wait_send()
+        copies_kernel[step].wait_send()
+
+
+def exchange(term_in, term_out, grad, local_kernel, factor, kernel_factor):
+    scenes, tiles = lax.axis_size("scene"), lax.axis_size("tile")
+    peers = scenes * tiles
+    steps = peers.bit_length() - 1
+    halo = KS // 2
+    height, breadth, channels = grad.shape
+    cut_in = (term_in.shape[0] // peers, term_in.shape[1])
+    cut_out = (term_out.shape[0] // peers, term_out.shape[1])
+    tall = {-1: halo, 0: height, 1: halo}
+    broad = {-1: halo, 0: breadth, 1: halo}
+    whole = pl.BlockSpec(memory_space=pltpu.VMEM)
+    results = pl.pallas_call(
+        functools.partial(exchange_body, scenes, tiles, factor, kernel_factor),
+        out_shape=[
+            jax.ShapeDtypeStruct(cut_in, jnp.float32),
+            jax.ShapeDtypeStruct(cut_out, jnp.float32),
+            jax.ShapeDtypeStruct(local_kernel.shape, jnp.float32),
+        ]
+        + [jax.ShapeDtypeStruct((tall[r], broad[c], channels), jnp.bfloat16) for r, c in SIDES],
+        in_specs=[whole] * 6,
+        out_specs=[whole] * 11,
+        scratch_shapes=[
+            pltpu.VMEM((2,) * (steps - 1 - k) + cut_in, jnp.bfloat16) for k in range(steps)
+        ]
+        + [pltpu.VMEM((2,) * (steps - 1 - k) + cut_out, jnp.bfloat16) for k in range(steps)]
+        + [
+            pltpu.VMEM((steps,) + local_kernel.shape, jnp.float32),
+            pltpu.VMEM((steps,) + local_kernel.shape, jnp.float32),
+            pltpu.SemaphoreType.DMA((3, steps)),
+            pltpu.SemaphoreType.DMA((3, steps)),
+            pltpu.SemaphoreType.DMA((8,)),
+            pltpu.SemaphoreType.DMA((8,)),
+        ],
+        compiler_params=pltpu.CompilerParams(
+            collective_id=0, has_side_effects=True, vmem_limit_bytes=48 * 2**20
+        ),
+    )(
+        term_in.reshape((2,) * steps + cut_in),
+        term_out.reshape((2,) * steps + cut_out),
+        grad,
+        grad[:, :halo],
+        grad[:, -halo:],
+        local_kernel,
+    )
+    w_in, w_out, kernel = results[:3]
+    around = dict(zip(SIDES, results[3:]))
+    around[(0, 0)] = grad
+    bands = [jnp.concatenate([around[(r, c)] for c in (-1, 0, 1)], axis=1) for r in (-1, 0, 1)]
+    return w_in, w_out, kernel, jnp.concatenate(bands, axis=0)
 
 
 def gelu_pair(hidden):
@@ -220,7 +439,16 @@
         - normed * jnp.mean(normed_grad * normed, axis=-1, keepdims=True)
     )
     mixed_low = mixed_grad.astype(jnp.bfloat16).reshape(height, breadth, channels)
-    grad_padded = extend(mixed_low)
+    factor = 1.0 / math.sqrt(tile_rows * peer_count)
+    kernel_factor = 1.0 / math.sqrt(GRID_W * GRID_W * tile_rows)
+    term_out = contract_rows(act_low, branch_grad).astype(jnp.bfloat16)
+    term_in = contract_rows(scaled, hidden_grad).astype(jnp.bfloat16)
+    local_kernel = lane_call(
+        terms_body, (mixed_low, padded), (KS, KS, channels), jnp.float32, padded.shape
+    )
+    grad_in, grad_out, grad_kernel, grad_padded = exchange(
+        term_in, term_out, mixed_low, local_kernel, factor, kernel_factor
+    )
     grad_input = lane_call(
         backward_body,
         (grad_padded, kernel, upstream.reshape(height, breadth, channels)),
@@ -228,28 +456,7 @@
         jnp.bfloat16,
         grad_padded.shape,
     )
-    factor = 1.0 / math.sqrt(tile_rows * peer_count)
-    kernel_factor = 1.0 / math.sqrt(GRID_W * GRID_W * tile_rows)
-    term_out = contract_rows(act_low, branch_grad).astype(jnp.bfloat16)
-    term_in = contract_rows(scaled, hidden_grad).astype(jnp.bfloat16)
-    first_out, first_in = (
-        lax.psum_scatter(term_out, "scene", scatter_dimension=0, tiled=True),
-        lax.psum_scatter(term_in, "scene", scatter_dimension=0, tiled=True),
-    )
-    grad_out, grad_in = (
-        lax.psum_scatter(first_out, "tile", scatter_dimension=0, tiled=True).astype(jnp.float32),
-        lax.psum_scatter(first_in, "tile", scatter_dimension=0, tiled=True).astype(jnp.float32),
-    )
-    local_kernel = lane_call(
-        terms_body, (mixed_low, padded), (KS, KS, channels), jnp.float32, padded.shape
-    )
-    grad_kernel = summed(local_kernel)
-    return (
-        grad_input.reshape(image.shape),
-        grad_in * factor,
-        grad_out * factor,
-        grad_kernel * kernel_factor,
-    )
+    return grad_input.reshape(image.shape), grad_in, grad_out, grad_kernel
 
 
 def solution(mesh):

time: 381 us -> 256 us (0.67)
  waiting for transfers between devices: 202 us -> 34.4 us
  Pallas kernels: 39 us -> 123 us
  starting transfers between devices: 34.1 us -> 15.7 us
  between operations: 14.2 us -> 0.98 us
  matrix products: 55.9 us -> 50.3 us
    reduce_scatter x4 -> x0, waiting for transfers between devices: 151 us -> none  [the longest x1 64.7 us: on_device(): lax.psum_scatter(first_out, 'tile', scatter_dimension=0, tiled=True)]
    pallas_call x0 -> x1, Pallas kernels: none -> 83.9 us  [exchange(): pl.pallas_call(functools.partial(exchange_body, scenes, tiles, factor, ke...]
    ppermute x5 -> x0, starting transfers between devices: 7.61 us -> none  [summed(): lax.ppermute(value, axis, [(d, d ^ bit) for d in range(count)])]
    ppermute x2 -> x1, waiting for transfers between devices: 15 us -> 8.93 us  [extend(): bottom = lax.ppermute(wide[:halo], 'tile', up_pairs)]
    dot_general x1, matrix products: 8.75 us -> 4.23 us  [on_device(): jnp.dot(hidden_grad, w_in.T, preferred_element_type=jnp.float32) * ln_gain]
    ppermute x5 -> x0, waiting for transfers between devices: 4.5 us -> none  [summed(): lax.ppermute(value, axis, [(d, d ^ bit) for d in range(count)])]
    ppermute x2 -> x1, starting transfers between devices: 8.82 us -> 4.5 us  [extend(): top = lax.ppermute(wide[-halo:], 'tile', down_pairs)]
    ppermute x2 -> x1, waiting for transfers between devices: 4.12 us -> 0.01 us  [extend(): right = lax.ppermute(block[:, :halo], 'tile', left_pairs)]
  transfers between devices with their start and end apart: 18 -> 5, of which waited for: 12 -> 3; matrix products, arithmetic and copies ran while one was open for 13% -> 9% of each run, Pallas kernels for 10% -> 5%
where the time goes in v2:
time: 256 us
  Pallas kernels  123 us (48%)
  matrix products  50.3 us (20%)
  waiting for transfers between devices  34.4 us (13%)
  starting transfers between devices  15.7 us (6%)
  other arithmetic  13.8 us (5%)
  blocking collectives  10.6 us (4%)
  local copies, waits for them, and re-layouts  7 us (3%)
    pallas_call x1, Pallas kernels, exchange(): pl.pallas_call(functools.partial(exchange_body, scenes, tiles, factor, ke...  83.9 us
    pallas_call x3, Pallas kernels, lane_call(): pl.pallas_call(body, out_shape=jax.ShapeDtypeStruct(out_shape, out_type),...  39.2 us
    all_to_all x1, waiting for transfers between devices, on_device(): lax.all_to_all(outgoing.reshape(peer_count, capacity, channels), ('scene'...  23.2 us
    dot_general x2, matrix products, contract_rows(): lax.dot_general(left_side, right_side, (((0,), (0,)), ((), ())), preferre...  17.6 us
    dot_general x1, matrix products, on_device(): act_grad = jnp.dot(branch_grad, w_out.T, preferred_element_type=jnp.float32)  11.3 us
    all_to_all x1, blocking collectives, on_device(): lax.all_to_all(targets.reshape(peer_count, capacity), ('scene', 'tile'),...  10.6 us
    ppermute x1, waiting for transfers between devices, extend(): bottom = lax.ppermute(wide[:halo], 'tile', up_pairs)  8.93 us
    dot_general x1, matrix products, on_device(): hidden = jnp.dot(scaled, w_in, preferred_element_type=jnp.float32) + bias_in  8.66 us
  transfers between devices with their start and end apart: 5, of which 3 were waited for; matrix products, arithmetic and copies ran while one was open for 9% of the time, Pallas kernels for 5%

profile of v2, /device:TPU:0, one launch (start us, length us, event | category | flops | bytes accessed | tf_op | source)
XLA Modules:
  0.0 255.9 jit_solution(4247112215387880894)
XLA Ops:
  0.6 0.0 copy-start
  0.6 1.3 fusion.24
  1.9 4.9 %collective-permute-start = (bf16[24,3,768]{2,1,0:T(4,128)(2,1)S(1)}, bf16[24,3,768]{2,1,0:T(4,128)(2,1)S(1)}, u32[]{:S(2)}, u32[]{:S(2)}) collective-permute-start(bf16[24,3,768]{2,1,0:T(4,128)(2,1)S(1)} %get-tuple-element.38), channel_id=1, source_target_pairs={{0,1},{1,2},{2,3},{4,5},{5,6},{6,7},{8,9},{9,10},{10,11},{12,13},{... | collective-permute-start | bytes 331784 | tf_op jit(solution)/shard_map/ppermute | solution.py:118
  6.8 1.3 collective-permute-start.1
  8.1 0.7 iota_add_fusion
  8.8 0.1 add.74
  8.9 0.7 iota_compare_fusion.3
  9.6 0.1 lt.29
  9.7 0.7 fusion.18
  10.4 0.0 copy-done
  10.4 0.0 copy-start.4
  10.5 4.6 %fusion.11 = bf16[1536,768]{1,0:T(8,128)(2,1)} fusion(bf16[832,768]{1,0:T(8,128)(2,1)S(1)} %copy-done, s32[1536]{0:T(1024)S(1)} %add.74, pred[1536]{0:T(1024)(128)(4,1)S(1)} %lt.29), kind=kOutput, calls=%fused_computation.18 | convolution fusion | flops 1966669824 | bytes 3644928 | tf_op jit(solution)/shard_map/dot_general | solution.py:398
  15.0 1.1 select_reduce_fusion
  16.1 0.0 collective-permute-done
  16.1 0.0 collective-permute-done.1
  16.1 0.0 copy-done.4
  16.1 0.0 copy-start.7
  16.1 0.1 pad_maximum_fusion.3
  16.3 4.5 %collective-permute-start.2 = (bf16[3,38,768]{2,1,0:T(8,128)(2,1)S(1)}, bf16[3,38,768]{2,1,0:T(8,128)(2,1)S(1)}, u32[]{:S(2)}, u32[]{:S(2)}) collective-permute-start(bf16[3,38,768]{2,1,0:T(8,128)(2,1)S(1)} %get-tuple-element.34), channel_id=1, source_target_pairs={{0,4},{1,5},{2,6},{3,7},{8,12},{9,13},{10,14},{11,15},{16,20},{17,... | collective-permute-start | bytes 525320 | tf_op jit(solution)/shard_map/ppermute | solution.py:121
  20.8 1.3 collective-permute-start.3
  22.1 0.0 copy-done.7
  22.1 0.0 copy-start.3
  22.1 2.3 collective-permute-done.2
  24.4 8.9 %collective-permute-done.3 = bf16[3,38,768]{2,1,0:T(8,128)(2,1)S(1)} collective-permute-done((bf16[3,38,768]{2,1,0:T(8,128)(2,1)S(1)}, bf16[3,38,768]{2,1,0:T(8,128)(2,1)S(1)}, u32[]{:S(2)}, u32[]{:S(2)}) %collective-permute-start.3) | collective-permute-done | bytes 175136 | tf_op jit(solution)/shard_map/ppermute | solution.py:122
  33.3 1.8 pad_maximum_fusion.padded_ref
  35.1 0.1 all_to_all.9
  35.2 10.6 %all_to_all.14 = s32[32,1,48]{2,1,0:T(1,128)S(1)} all-to-all(s32[32,1,48]{2,1,0:T(1,128)S(1)} %all_to_all.9), channel_id=1, replica_groups=mesh['scene'=4,'tile'=8] {'scene','tile'}, dimensions={0} | all-to-all | bytes 12288 | tf_op jit(solution)/shard_map/all_to_all | solution.py:411
  45.8 3.7 %all-to-all-start.1 = ((bf16[32,48,768]{2,1,0:T(8,128)(2,1)}), bf16[32,48,768]{2,1,0:T(8,128)(2,1)}, u32[]{:S(2)}, u32[]{:S(2)}) async-start(bf16[32,48,768]{2,1,0:T(8,128)(2,1)} %bitcast.39), calls=%async_computation.1 | async-start | bytes 4718592 | tf_op jit(solution)/shard_map/all_to_all | solution.py:407
  49.5 0.0 copy-done.3
  49.5 13.9 %shard_map.138 = f32[24,32,768]{2,1,0:T(8,128)S(1)} custom-call(bf16[30,38,768]{2,1,0:T(8,128)(2,1)S(1)} %pad_maximum_fusion.padded_ref, f32[7,7,768]{2,1,0:T(8,128)S(1)} %copy-done.3), custom_call_target="tpu_custom_call" | custom-call | flops 8580096000 | bytes 41943040 | tf_op jit(solution)/shard_map/pallas_call | solution.py:99
  63.4 0.0 copy-start.1
  63.4 1.5 copy-done.1
  64.9 1.9 reduce_sum.46
  66.7 0.1 div.15
  66.8 2.0 multiply_reduce_fusion.1
  68.9 0.1 rsqrt.12
  68.9 0.0 copy-done.8
  69.0 2.0 multiply_convert_fusion.4
  71.0 0.0 copy-start.5
  71.0 1.0 copy-done.5
  72.0 8.7 %fusion.25 = f32[768,3072]{1,0:T(8,128)} fusion(bf16[768,768]{1,0:T(8,128)(2,1)S(1)} %multiply_convert_fusion.4, bf16[768,3072]{1,0:T(8,128)(2,1)} %param.14), kind=kOutput, calls=%fused_computation.50 | convolution fusion | flops 3623878656 | bytes 15335424 | tf_op jit(solution)/shard_map/dot_general | solution.py:425
  80.7 0.5 broadcast.91
  81.2 0.7 reduce.5
  81.9 0.1 eq.34
  81.9 23.2 %all-to-all-done.1 = bf16[32,48,768]{2,1,0:T(8,128)(2,1)} async-done(((bf16[32,48,768]{2,1,0:T(8,128)(2,1)}), bf16[32,48,768]{2,1,0:T(8,128)(2,1)}, u32[]{:S(2)}, u32[]{:S(2)}) %all-to-all-start.1) | async-done | bytes 2359328 | tf_op jit(solution)/shard_map/all_to_all | solution.py:407
  105.1 4.0 %fusion.10 = f32[768,768]{1,0:T(8,128)S(1)} fusion(bf16[1536,768]{1,0:T(8,128)(2,1)} %bitcast.5, s32[1536]{0:T(1024)S(1)} %eq.34), kind=kOutput, calls=%fused_computation.17 | convolution fusion | flops 1813118976 | bytes 4724736 | tf_op jit(solution)/shard_map/dot_general | solution.py:431
  109.1 0.0 copy-done.9
  109.1 0.0 copy-done.10
  109.1 0.0 copy-start.2
  109.1 0.0 slice-start.1
  109.1 11.3 %fusion.6 = bf16[768,3072]{1,0:T(8,128)(2,1)S(1)} fusion(f32[768,3072]{1,0:T(8,128)} %fusion.25, bf16[3072,768]{1,0:T(8,128)(2,1)} %param.16, f32[3072]{0:T(1024)S(1)} %copy-done.9, f32[768,768]{1,0:T(8,128)S(1)} %fusion.10, f32[768]{0:T(1024)S(1)} %copy-done.10), kind=kOutput, calls=%fused_computation.8 | convolution fusion | flops 3672244224 | bytes 21249024 | tf_op jit(solution)/shard_map/dot_general | solution.py:433
  120.4 4.2 %multiply_reduce_fusion.2 = (f32[768]{0:T(1024)S(1)}, f32[768]{0:T(1024)S(1)}, f32[768,768]{1,0:T(8,128)S(1)}) fusion(f32[768]{0:T(1024)S(1)} %copy-done.8, f32[768]{0:T(1024)S(1)} %rsqrt.12, f32[768]{0:T(1024)S(1)} %div.15, f32[24,32,768]{2,1,0:T(8,128)S(1)} %copy-done.2, bf16[768,3072]{1,0:T(8,128)(2,1)S(1)} %fusion.6, bf16[768,3072]{1,0:T(8,128)(2,1)S(1)} %bitcast.43), kind=kOutput, calls=%fused_computation.29 | convolution fusion | flops 3627416064 | bytes 14171136 | tf_op jit(solution)/shard_map/dot_general | solution.py:435
  124.7 0.9 multiply_convert_fusion.2
  125.6 11.6 %shard_map.139.local_ref = f32[7,7,768]{2,1,0:T(8,128)S(1)} custom-call(bf16[24,32,768]{2,1,0:T(8,128)(2,1)S(1)} %bitcast.29, bf16[30,38,768]{2,1,0:T(8,128)(2,1)S(1)} %pad_maximum_fusion.padded_ref), custom_call_target="tpu_custom_call" | custom-call | flops 8580096000 | bytes 41943040 | tf_op jit(solution)/shard_map/pallas_call | solution.py:99
  137.2 0.1 fusion.23
  137.3 0.0 copy-start.6
  137.3 12.0 %convolution_convert_fusion = bf16[3072,768]{1,0:T(8,128)(2,1)} fusion(f32[768,3072]{1,0:T(8,128)} %fusion.25, f32[3072]{0:T(1024)S(1)} %copy-done.9, f32[768,768]{1,0:T(8,128)S(1)} %fusion.10, f32[768]{0:T(1024)S(1)} %copy-done.10), kind=kOutput, calls=%fused_computation.14 | convolution fusion | flops 3651010560 | bytes 16530432 | tf_op jit(solution)/shard_map/dot_general | solution.py:365
  149.3 5.7 %convolution_convert_fusion.1 = bf16[768,3072]{1,0:T(8,128)(2,1)} fusion(bf16[768,768]{1,0:T(8,128)(2,1)S(1)} %copy-done.6, bf16[768,3072]{1,0:T(8,128)(2,1)S(1)} %fusion.6), kind=kOutput, calls=%fused_computation.15 | convolution fusion | flops 3626237952 | bytes 10616832 | tf_op jit(solution)/shard_map/dot_general | solution.py:365
  155.0 83.9 %shard_map.140 = (f32[24,3072]{1,0:T(8,128)S(1)}, f32[96,768]{1,0:T(8,128)S(1)}, f32[7,7,768]{2,1,0:T(8,128)S(1)}, bf16[3,3,768]{2,1,0:T(4,128)(2,1)S(1)}, bf16[...) custom-call(bf16[2,2,2,2,2,24,3072]{6,5,4,3,2,1,0:T(8,128)(2,1)} %bi, ...), custom_call_target="tpu_custom_call" | custom-call | tf_op jit(solution)/shard_map/pallas_call | solution.py:314
  238.9 1.2 maximum_maximum_fusion.padded_ref
  240.1 13.7 %shard_map.141 = bf16[24,32,768]{2,1,0:T(8,128)(2,1)} custom-call(bf16[30,38,768]{2,1,0:T(8,128)(2,1)S(1)} %maximum_maximum_fusion.padded_ref, f32[7,7,768]{2,1,0:T(8,128)S(1)} %copy-done.3, f32[24,32,768]{2,1,0:T(8,128)S(1)} %bitcast.33), custom_call_target="tpu_custom_call" | custom-call | flops 8580096000 | bytes 41943040 | tf_op jit(solution)/shard_map/pallas_call | solution.py:99
  253.8 0.7 copy.18
  254.5 0.7 copy.19
  255.2 0.7 copy.20
  (13 shorter events, 0.0 us)
Async XLA Ops:
  0.6 9.8 %copy-start = (bf16[832,768]{1,0:T(8,128)(2,1)S(1)}, bf16[832,768]{1,0:T(8,128)(2,1)}, u32[]{:S(2)}) copy-start(bf16[832,768]{1,0:T(8,128)(2,1)} %param.18) | copy-start | bytes 3833860
  1.9 14.2 %collective-permute-start = (bf16[24,3,768]{2,1,0:T(4,128)(2,1)S(1)}, bf16[24,3,768]{2,1,0:T(4,128)(2,1)S(1)}, u32[]{:S(2)}, u32[]{:S(2)}) collective-permute-start(bf16[24,3,768]{2,1,0:T(4,128)(2,1)S(1)} %get-tuple-element.38), channel_id=1, source_target_pairs={{0,1},{1,2},{2,3},{4,5},{5,6},{6,7},{8,9},{9,10},{10,11},{12,13},{... | collective-permute-start | bytes 331784 | tf_op jit(solution)/shard_map/ppermute | solution.py:118
  6.8 9.3 %collective-permute-start.1 = (bf16[24,3,768]{2,1,0:T(4,128)(2,1)S(1)}, bf16[24,3,768]{2,1,0:T(4,128)(2,1)S(1)}, u32[]{:S(2)}, u32[]{:S(2)}) collective-permute-start(bf16[24,3,768]{2,1,0:T(4,128)(2,1)S(1)} %get-tuple-element.39), channel_id=1, source_target_pairs={{1,0},{2,1},{3,2},{5,4},{6,5},{7,6},{9,8},{10,9},{11,10},{13,12},{... | collective-permute-start | bytes 331784 | tf_op jit(solution)/shard_map/ppermute | solution.py:119
  10.4 5.7 %copy-start.4 = (bf16[1,1,24,32,768]{4,3,2,1,0:T(8,128)(2,1)S(1)}, bf16[1,1,24,32,768]{4,3,2,1,0:T(8,128)(2,1)}, u32[]{:S(2)}) copy-start(bf16[1,1,24,32,768]{4,3,2,1,0:T(8,128)(2,1)} %param.11) | copy-start | bytes 3538948
  16.1 6.0 %copy-start.7 = (bf16[24,3,768]{2,1,0:T(4,128)(2,1)}, bf16[24,3,768]{2,1,0:T(4,128)(2,1)S(1)}, u32[]{:S(2)}) copy-start(bf16[24,3,768]{2,1,0:T(4,128)(2,1)S(1)} %collective-permute-done.1) | copy-start | bytes 331780
  16.3 8.1 %collective-permute-start.2 = (bf16[3,38,768]{2,1,0:T(8,128)(2,1)S(1)}, bf16[3,38,768]{2,1,0:T(8,128)(2,1)S(1)}, u32[]{:S(2)}, u32[]{:S(2)}) collective-permute-start(bf16[3,38,768]{2,1,0:T(8,128)(2,1)S(1)} %get-tuple-element.34), channel_id=1, source_target_pairs={{0,4},{1,5},{2,6},{3,7},{8,12},{9,13},{10,14},{11,15},{16,20},{17,... | collective-permute-start | bytes 525320 | tf_op jit(solution)/shard_map/ppermute | solution.py:121
  20.8 12.6 %collective-permute-start.3 = (bf16[3,38,768]{2,1,0:T(8,128)(2,1)S(1)}, bf16[3,38,768]{2,1,0:T(8,128)(2,1)S(1)}, u32[]{:S(2)}, u32[]{:S(2)}) collective-permute-start(bf16[3,38,768]{2,1,0:T(8,128)(2,1)S(1)} %get-tuple-element.35), channel_id=1, source_target_pairs={{4,0},{5,1},{6,2},{7,3},{12,8},{13,9},{14,10},{15,11},{20,16},{21,... | collective-permute-start | bytes 525320 | tf_op jit(solution)/shard_map/ppermute | solution.py:122
  22.1 27.4 %copy-start.3 = (f32[7,7,768]{2,1,0:T(8,128)S(1)}, f32[7,7,768]{2,1,0:T(8,128)}, u32[]{:S(2)}) copy-start(f32[7,7,768]{2,1,0:T(8,128)} %kernel_ref.3) | copy-start | bytes 451588
  45.8 59.3 %all-to-all-start.1 = ((bf16[32,48,768]{2,1,0:T(8,128)(2,1)}), bf16[32,48,768]{2,1,0:T(8,128)(2,1)}, u32[]{:S(2)}, u32[]{:S(2)}) async-start(bf16[32,48,768]{2,1,0:T(8,128)(2,1)} %bitcast.39), calls=%async_computation.1 | async-start | bytes 4718592 | tf_op jit(solution)/shard_map/all_to_all | solution.py:407
  63.4 1.5 copy-start.1
  64.9 4.1 %copy-start.8 = (f32[768]{0:T(1024)S(1)}, f32[768]{0:T(1024)}, u32[]{:S(2)}) copy-start(f32[768]{0:T(1024)} %param.13) | copy-start | bytes 9220
  71.0 1.0 copy-start.5
  105.1 4.0 %copy-start.9 = (f32[3072]{0:T(1024)S(1)}, f32[3072]{0:T(1024)}, u32[]{:S(2)}) copy-start(f32[3072]{0:T(1024)} %param.15) | copy-start | bytes 36868
  105.1 4.0 %copy-start.10 = (f32[768]{0:T(1024)S(1)}, f32[768]{0:T(1024)}, u32[]{:S(2)}) copy-start(f32[768]{0:T(1024)} %param.17) | copy-start | bytes 9220
  105.1 15.3 %slice-start = ((s8[4718592]{0:T(1024)(128)(4,1)}), s8[4194304]{0:T(1024)(128)(4,1)S(1)}, s32[]{:S(2)}) async-start(s8[4718592]{0:T(1024)(128)(4,1)} %bitcast.42), calls=%async_computation.2 | async-start | bytes 8388608
  109.1 11.3 %copy-start.2 = (f32[24,32,768]{2,1,0:T(8,128)S(1)}, f32[24,32,768]{2,1,0:T(8,128)}, u32[]{:S(2)}) copy-start(f32[24,32,768]{2,1,0:T(8,128)} %copy-done.1) | copy-start | bytes 7077892
  109.1 11.3 %slice-start.1 = ((s8[4718592]{0:T(1024)(128)(4,1)}), s8[524288]{0:T(1024)(128)(4,1)S(1)}, s32[]{:S(2)}) async-start(s8[4718592]{0:T(1024)(128)(4,1)} %bitcast.42), calls=%async_computation.3 | async-start | bytes 1048576
  137.3 12.0 %copy-start.6 = (bf16[768,768]{1,0:T(8,128)(2,1)S(1)}, bf16[768,768]{1,0:T(8,128)(2,1)}, u32[]{:S(2)}) copy-start(bf16[768,768]{1,0:T(8,128)(2,1)} %copy-done.5) | copy-start | bytes 3538948

commit v3 on v2

--- a/solution.py
+++ b/solution.py
@@ -54,9 +54,8 @@
             out_ref[first + out] = sums[out]
 
 
-def backward_body(padded_ref, kernel_ref, up_ref, out_ref, wide_ref):
+def backward_part(wide_ref, kernel_ref, up_ref, out_ref):
     height, breadth = out_ref.shape[0], out_ref.shape[1]
-    widen(padded_ref, wide_ref)
 
     @pl.loop(0, height // GROUP)
     def _(group):
@@ -108,21 +107,6 @@
     )(*args)
 
 
-def extend(block):
-    halo = KS // 2
-    tiles = lax.axis_size("tile")
-    right_pairs = [(t, t + 1) for t in range(tiles) if t % GRID_W < GRID_W - 1]
-    left_pairs = [(b, a) for a, b in right_pairs]
-    down_pairs = [(t, t + GRID_W) for t in range(tiles - GRID_W)]
-    up_pairs = [(b, a) for a, b in down_pairs]
-    left = lax.ppermute(block[:, -halo:], "tile", right_pairs)
-    right = lax.ppermute(block[:, :halo], "tile", left_pairs)
-    wide = jnp.concatenate([left, block, right], axis=1)
-    top = lax.ppermute(wide[-halo:], "tile", down_pairs)
-    bottom = lax.ppermute(wide[:halo], "tile", up_pairs)
-    return jnp.concatenate([top, wide, bottom], axis=0)
-
-
 MESH = pl.DeviceIdType.MESH
 SIDES = [(r, c) for r in (-1, 0, 1) for c in (-1, 0, 1) if (r, c) != (0, 0)]
 
@@ -135,17 +119,143 @@
     return [("scene", bit) for bit in bits_of(scenes)] + [("tile", bit) for bit in bits_of(tiles)]
 
 
+class Halo:
+    def __init__(self, tiles, block_ref, first_ref, last_ref, pieces, send, recv):
+        tile = lax.axis_index("tile")
+        self.tile, self.pieces, self.send, self.recv = tile, pieces, send, recv
+        self.block, self.first, self.last = block_ref, first_ref, last_ref
+        row, col = tile // GRID_W, lax.rem(tile, GRID_W)
+        self.there = [
+            (row + r >= 0) & (row + r < tiles // GRID_W) & (col + c >= 0) & (col + c < GRID_W)
+            for r, c in SIDES
+        ]
+
+    def neighbour(self, number):
+        row, col = SIDES[number]
+        return {"tile": self.tile + row * GRID_W + col}
+
+    def greet(self, barrier):
+        for number in range(8):
+
+            @pl.when(self.there[number])
+            def _():
+                pl.semaphore_signal(
+                    barrier, inc=1, device_id=self.neighbour(number), device_id_type=MESH
+                )
+
+        return sum(jnp.where(there, 1, 0).astype(jnp.int32) for there in self.there)
+
+    def copy(self, number):
+        row, col = SIDES[number]
+        source = {-1: self.first, 0: self.block, 1: self.last}[col]
+        width = KS // 2
+        if row == -1:
+            source = source.at[pl.ds(0, width)]
+        elif row == 1:
+            source = source.at[pl.ds(self.block.shape[0] - width, width)]
+        landing = SIDES.index((-row, -col))
+        return pltpu.make_async_remote_copy(
+            src_ref=source,
+            dst_ref=self.pieces[landing],
+            send_sem=self.send.at[number],
+            recv_sem=self.recv.at[landing],
+            device_id=self.neighbour(number),
+            device_id_type=MESH,
+        )
+
+    def arrival(self, number):
+        return pltpu.make_async_remote_copy(
+            src_ref=self.pieces[number],
+            dst_ref=self.pieces[number],
+            send_sem=self.send.at[number],
+            recv_sem=self.recv.at[number],
+            device_id=self.neighbour(number),
+            device_id_type=MESH,
+        )
+
+    def start(self):
+        for number in range(8):
+
+            @pl.when(self.there[number])
+            def _():
+                self.copy(number).start()
+
+    def finish(self):
+        for number in range(8):
+            piece = self.pieces[number]
+
+            @pl.when(self.there[number])
+            def _():
+                self.copy(number).wait_send()
+                self.arrival(number).wait_recv()
+
+            @pl.when(jnp.logical_not(self.there[number]))
+            def _():
+                piece[...] = jnp.zeros(piece.shape, piece.dtype)
+
+    def assemble(self, lanes, wide_ref):
+        height, breadth = self.block.shape[0], self.block.shape[1]
+        width = KS // 2
+        parts = dict(zip(SIDES, self.pieces))
+        parts[(0, 0)] = self.block
+        for row, first, count in ((-1, 0, width), (0, width, height), (1, width + height, width)):
+
+            @pl.loop(0, count)
+            def _(line):
+                for col, place, size in (
+                    (-1, 0, width), (0, width, breadth), (1, width + breadth, width)
+                ):
+                    wide_ref[first + line, pl.ds(place, size), :] = parts[(row, col)][
+                        line, :, lanes
+                    ].astype(jnp.float32)
+
+
+def halo_shapes(shape):
+    halo = KS // 2
+    tall = {-1: halo, 0: shape[0], 1: halo}
+    broad = {-1: halo, 0: shape[1], 1: halo}
+    return [(tall[r], broad[c], shape[2]) for r, c in SIDES]
+
+
+def halo_body(tiles, block_ref, first_ref, last_ref, *rest):
+    halo = Halo(tiles, block_ref, first_ref, last_ref, rest[:8], rest[8], rest[9])
+    barrier = pltpu.get_barrier_semaphore()
+    pl.semaphore_wait(barrier, halo.greet(barrier))
+    halo.start()
+    halo.finish()
+
+
+def extend(block):
+    width = KS // 2
+    whole = pl.BlockSpec(memory_space=pltpu.VMEM)
+    results = pl.pallas_call(
+        functools.partial(halo_body, lax.axis_size("tile")),
+        out_shape=[jax.ShapeDtypeStruct(shape, jnp.bfloat16) for shape in halo_shapes(block.shape)],
+        in_specs=[whole] * 3,
+        out_specs=[whole] * 8,
+        scratch_shapes=[pltpu.SemaphoreType.DMA((8,)), pltpu.SemaphoreType.DMA((8,))],
+        compiler_params=pltpu.CompilerParams(
+            collective_id=1, has_side_effects=True, vmem_limit_bytes=16 * 2**20
+        ),
+    )(block, block[:, :width], block[:, -width:])
+    around = dict(zip(SIDES, results))
+    around[(0, 0)] = block
+    bands = [jnp.concatenate([around[(r, c)] for c in (-1, 0, 1)], axis=1) for r in (-1, 0, 1)]
+    return jnp.concatenate(bands, axis=0)
+
+
 def exchange_body(
     scenes, tiles, factor, kernel_factor,
-    in_ref, out_ref, grad_ref, first_ref, last_ref, local_ref,
-    w_in_ref, w_out_ref, kernel_ref, *rest,
+    in_ref, out_ref, grad_ref, first_ref, last_ref, padded_ref, taps_ref, up_ref,
+    w_in_ref, w_out_ref, kernel_ref, image_ref, *rest,
 ):
     places = place_of(scenes, tiles)
     steps = len(places)
     halos = rest[:8]
     rest = rest[8:]
     got_in, got_out = rest[:steps], rest[steps : 2 * steps]
-    got_kernel, sent_kernel, send_sems, recv_sems, halo_send, halo_recv = rest[2 * steps :]
+    got_kernel, sent_kernel, send_sems, recv_sems, halo_send, halo_recv, wide_ref = rest[2 * steps :]
+    halo = Halo(tiles, grad_ref, first_ref, last_ref, halos, halo_send, halo_recv)
     me = {"scene": lax.axis_index("scene"), "tile": lax.axis_index("tile")}
     scene_bits = [p for p in places if p[0] == "scene"][::-1]
     tile_bits = [p for p in places if p[0] == "tile"][::-1]
@@ -158,27 +268,10 @@
     def partner(place):
         return {place[0]: me[place[0]] + place[1] * (1 - 2 * half(place))}
 
-    grid_row, grid_col = me["tile"] // GRID_W, lax.rem(me["tile"], GRID_W)
-
-    def present(side):
-        row, col = grid_row + side[0], grid_col + side[1]
-        return (row >= 0) & (row < tiles // GRID_W) & (col >= 0) & (col < GRID_W)
-
-    def neighbour(side):
-        return {"tile": me["tile"] + side[0] * GRID_W + side[1]}
-
     barrier = pltpu.get_barrier_semaphore()
     for place in places:
         pl.semaphore_signal(barrier, inc=1, device_id=partner(place), device_id_type=MESH)
-    for side in SIDES:
-
-        @pl.when(present(side))
-        def _():
-            pl.semaphore_signal(barrier, inc=1, device_id=neighbour(side), device_id_type=MESH)
-
-    pl.semaphore_wait(
-        barrier, steps + sum(jnp.where(present(side), 1, 0).astype(jnp.int32) for side in SIDES)
-    )
+    pl.semaphore_wait(barrier, steps + halo.greet(barrier))
 
     def position(order, step):
         left = [p for p in places if p not in order[:step]]
@@ -226,46 +319,32 @@
             device_id_type=MESH,
         )
 
-    def halo_copy(number):
-        row, col = SIDES[number]
-        source = {-1: first_ref, 0: grad_ref, 1: last_ref}[col]
-        width = KS // 2
-        if row == -1:
-            source = source.at[pl.ds(0, width)]
-        elif row == 1:
-            source = source.at[pl.ds(grad_ref.shape[0] - width, width)]
-        return pltpu.make_async_remote_copy(
-            src_ref=source,
-            dst_ref=halos[SIDES.index((-row, -col))],
-            send_sem=halo_send.at[number],
-            recv_sem=halo_recv.at[SIDES.index((-row, -col))],
-            device_id=neighbour((row, col)),
-            device_id_type=MESH,
+    def each_lane(work):
+        @pl.loop(0, grad_ref.shape[2] // LANES)
+        def _(lane):
+            work(pl.ds(pl.multiple_of(lane * LANES, LANES), LANES))
+
+    def kernel_part(lanes):
+        terms_body(
+            grad_ref.at[:, :, lanes],
+            padded_ref.at[:, :, lanes],
+            sent_kernel.at[0, :, :, lanes],
+            wide_ref,
         )
 
-    def halo_arrival(number):
-        row, col = SIDES[number]
-        return pltpu.make_async_remote_copy(
-            src_ref=halos[number],
-            dst_ref=halos[number],
-            send_sem=halo_send.at[number],
-            recv_sem=halo_recv.at[number],
-            device_id=neighbour((row, col)),
-            device_id_type=MESH,
+    def image_part(lanes):
+        halo.assemble(lanes, wide_ref)
+        backward_part(
+            wide_ref, taps_ref.at[:, :, lanes], up_ref.at[:, :, lanes], image_ref.at[:, :, lanes]
         )
-
-    for number in range(8):
-
-        @pl.when(present(SIDES[number]))
-        def _():
-            halo_copy(number).start()
 
     copies_in = [weight_copy(0, order_in, in_ref, got_in, step) for step in range(steps)]
     copies_out = [weight_copy(1, order_out, out_ref, got_out, step) for step in range(steps)]
     copies_kernel = [kernel_copy(step) for step in range(steps)]
     copies_in[0].start()
     copies_out[0].start()
-    sent_kernel[0] = local_ref[...]
+    halo.start()
+    each_lane(kernel_part)
     copies_kernel[0].start()
     for step in range(steps):
         later = step < steps - 1
@@ -283,24 +362,16 @@
             copies_kernel[step + 1].start()
         else:
             kernel_ref[...] = (sent_kernel[step] + got_kernel[step]) * kernel_factor
-    for number in range(8):
-
-        @pl.when(present(SIDES[number]))
-        def _():
-            halo_copy(number).wait_send()
-            halo_arrival(number).wait_recv()
-
-        @pl.when(jnp.logical_not(present(SIDES[number])))
-        def _():
-            halos[number][...] = jnp.zeros(halos[number].shape, halos[number].dtype)
-
+        if step == 0:
+            halo.finish()
+            each_lane(image_part)
     for step in range(steps):
         copies_in[step].wait_send()
         copies_out[step].wait_send()
         copies_kernel[step].wait_send()
 
 
-def exchange(term_in, term_out, grad, local_kernel, factor, kernel_factor):
+def exchange(term_in, term_out, grad, padded, kernel, upstream, factor, kernel_factor):
     scenes, tiles = lax.axis_size("scene"), lax.axis_size("tile")
     peers = scenes * tiles
     steps = peers.bit_length() - 1
@@ -308,30 +379,30 @@
     height, breadth, channels = grad.shape
     cut_in = (term_in.shape[0] // peers, term_in.shape[1])
     cut_out = (term_out.shape[0] // peers, term_out.shape[1])
-    tall = {-1: halo, 0: height, 1: halo}
-    broad = {-1: halo, 0: breadth, 1: halo}
     whole = pl.BlockSpec(memory_space=pltpu.VMEM)
     results = pl.pallas_call(
         functools.partial(exchange_body, scenes, tiles, factor, kernel_factor),
         out_shape=[
             jax.ShapeDtypeStruct(cut_in, jnp.float32),
             jax.ShapeDtypeStruct(cut_out, jnp.float32),
-            jax.ShapeDtypeStruct(local_kernel.shape, jnp.float32),
-        ]
-        + [jax.ShapeDtypeStruct((tall[r], broad[c], channels), jnp.bfloat16) for r, c in SIDES],
-        in_specs=[whole] * 6,
-        out_specs=[whole] * 11,
-        scratch_shapes=[
+            jax.ShapeDtypeStruct(kernel.shape, jnp.float32),
+            jax.ShapeDtypeStruct(grad.shape, jnp.bfloat16),
+        ],
+        in_specs=[whole] * 8,
+        out_specs=[whole] * 4,
+        scratch_shapes=[pltpu.VMEM(shape, jnp.bfloat16) for shape in halo_shapes(grad.shape)]
+        + [
             pltpu.VMEM((2,) * (steps - 1 - k) + cut_in, jnp.bfloat16) for k in range(steps)
         ]
         + [pltpu.VMEM((2,) * (steps - 1 - k) + cut_out, jnp.bfloat16) for k in range(steps)]
         + [
-            pltpu.VMEM((steps,) + local_kernel.shape, jnp.float32),
-            pltpu.VMEM((steps,) + local_kernel.shape, jnp.float32),
+            pltpu.VMEM((steps,) + kernel.shape, jnp.float32),
+            pltpu.VMEM((steps,) + kernel.shape, jnp.float32),
             pltpu.SemaphoreType.DMA((3, steps)),
             pltpu.SemaphoreType.DMA((3, steps)),
             pltpu.SemaphoreType.DMA((8,)),
             pltpu.SemaphoreType.DMA((8,)),
+            pltpu.VMEM((height + 2 * halo, -(-(breadth + 2 * halo) // 8) * 8, LANES), jnp.float32),
         ],
         compiler_params=pltpu.CompilerParams(
             collective_id=0, has_side_effects=True, vmem_limit_bytes=48 * 2**20
@@ -342,13 +413,11 @@
         grad,
         grad[:, :halo],
         grad[:, -halo:],
-        local_kernel,
-    )
-    w_in, w_out, kernel = results[:3]
-    around = dict(zip(SIDES, results[3:]))
-    around[(0, 0)] = grad
-    bands = [jnp.concatenate([around[(r, c)] for c in (-1, 0, 1)], axis=1) for r in (-1, 0, 1)]
-    return w_in, w_out, kernel, jnp.concatenate(bands, axis=0)
+        padded,
+        kernel,
+        upstream,
+    )
+    return results
 
 
 def gelu_pair(hidden):
@@ -402,17 +471,14 @@
     targets = jnp.sum(jnp.where(chosen, local_places[None, :], 0), axis=1) - 1
     own_block = image[0, 0]
     padded = extend(own_block)
-    outgoing, targets, padded = lax.optimization_barrier((outgoing, targets, padded))
-    arrived, places = (
-        lax.all_to_all(
-            outgoing.reshape(peer_count, capacity, channels),
-            ("scene", "tile"), split_axis=0, concat_axis=0, tiled=True,
-        ),
-        lax.all_to_all(
-            targets.reshape(peer_count, capacity),
-            ("scene", "tile"), split_axis=0, concat_axis=0, tiled=True,
-        ),
-    )
+    outgoing, padded = lax.optimization_barrier((outgoing, padded))
+    arrived = lax.all_to_all(
+        outgoing.reshape(peer_count, capacity, channels),
+        ("scene", "tile"), split_axis=0, concat_axis=0, tiled=True,
+    )
+    everyone = lax.all_gather(targets.reshape(1, peer_count * capacity), ("scene", "tile"), tiled=True)
+    mine = lax.axis_index(("scene", "tile")) * capacity
+    places = lax.dynamic_slice_in_dim(everyone, mine, capacity, axis=1)
     arrived = arrived.reshape(-1, channels)
     places = places.reshape(-1)
     mixed_sum = lane_call(
@@ -443,18 +509,15 @@
     kernel_factor = 1.0 / math.sqrt(GRID_W * GRID_W * tile_rows)
     term_out = contract_rows(act_low, branch_grad).astype(jnp.bfloat16)
     term_in = contract_rows(scaled, hidden_grad).astype(jnp.bfloat16)
-    local_kernel = lane_call(
-        terms_body, (mixed_low, padded), (KS, KS, channels), jnp.float32, padded.shape
-    )
-    grad_in, grad_out, grad_kernel, grad_padded = exchange(
-        term_in, term_out, mixed_low, local_kernel, factor, kernel_factor
-    )
-    grad_input = lane_call(
-        backward_body,
-        (grad_padded, kernel, upstream.reshape(height, breadth, channels)),
-        (height, breadth, channels),
-        jnp.bfloat16,
-        grad_padded.shape,
+    grad_in, grad_out, grad_kernel, grad_input = exchange(
+        term_in,
+        term_out,
+        mixed_low,
+        padded,
+        kernel,
+        upstream.reshape(height, breadth, channels),
+        factor,
+        kernel_factor,
     )
     return grad_input.reshape(image.shape), grad_in, grad_out, grad_kernel
 

time: 256 us -> 279 us (1.090); the launches traced: 256 us -> 276 us
  blocking collectives: 10.6 us -> 92.5 us
  waiting for transfers between devices: 34.4 us -> 0.01 us
  Pallas kernels: 123 us -> 107 us
  starting transfers between devices: 15.7 us -> 5.83 us
  other arithmetic: 13.8 us -> 10.5 us
    all_gather x0 -> x1, blocking collectives: none -> 92.5 us  [on_device(): lax.all_gather(targets.reshape(1, peer_count * capacity), ('scene', 'tile...]
    pallas_call x3 -> x1, Pallas kernels: 39.2 us -> 11.2 us  [lane_call(): pl.pallas_call(body, out_shape=jax.ShapeDtypeStruct(out_shape, out_type),...]
    all_to_all x1, waiting for transfers between devices: 23.2 us -> 0.01 us  [on_device(): lax.all_to_all(outgoing.reshape(peer_count, capacity, channels), ('scene'...]
    pallas_call x0 -> x1, Pallas kernels: none -> 13.4 us  [extend(): pl.pallas_call(functools.partial(halo_body, lax.axis_size('tile')), out_s...]
    ppermute x4 -> x0, starting transfers between devices: 12 us -> none  [the longest x1 4.88 us: extend(): left = lax.ppermute(block[:, -halo:], 'tile', right_pairs)]
    ppermute x4 -> x0, waiting for transfers between devices: 11.2 us -> none  [the longest x1 8.93 us: extend(): bottom = lax.ppermute(wide[:halo], 'tile', up_pairs)]
    all_to_all x1 -> x0, blocking collectives: 10.6 us -> none  [on_device(): lax.all_to_all(targets.reshape(peer_count, capacity), ('scene', 'tile'),...]
    unnamed x29 -> x39, local copies, waits for them, and re-layouts: 4.63 us -> 6.88 us
  transfers between devices with their start and end apart: 5 -> 1, of which waited for: 3 -> 0; matrix products, arithmetic and copies ran while one was open for 9% -> 6% of each run, Pallas kernels for 5% -> 4%
where the time goes in v3:
time: 279 us; the launch traced here: 276 us
  Pallas kernels  107 us (38%)
  blocking collectives  92.5 us (33%)
  matrix products  49.7 us (18%)
  other arithmetic  10.5 us (4%)
  local copies, waits for them, and re-layouts  8.77 us (3%)
  starting transfers between devices  5.83 us (2%)
    all_gather x1, blocking collectives, on_device(): lax.all_gather(targets.reshape(1, peer_count * capacity), ('scene', 'tile...  92.5 us
    pallas_call x1, Pallas kernels, exchange(): pl.pallas_call(functools.partial(exchange_body, scenes, tiles, factor, ke...  82.8 us
    dot_general x2, matrix products, contract_rows(): lax.dot_general(left_side, right_side, (((0,), (0,)), ((), ())), preferre...  18.4 us
    pallas_call x1, Pallas kernels, extend(): pl.pallas_call(functools.partial(halo_body, lax.axis_size('tile')), out_s...  13.4 us
    pallas_call x1, Pallas kernels, lane_call(): pl.pallas_call(body, out_shape=jax.ShapeDtypeStruct(out_shape, out_type),...  11.2 us
    dot_general x1, matrix products, on_device(): act_grad = jnp.dot(branch_grad, w_out.T, preferred_element_type=jnp.float32)  10.1 us
    dot_general x1, matrix products, on_device(): hidden = jnp.dot(scaled, w_in, preferred_element_type=jnp.float32) + bias_in  8.52 us
    unnamed x39, local copies, waits for them, and re-layouts  6.88 us
  transfers between devices with their start and end apart: 1, of which 0 were waited for; matrix products, arithmetic and copies ran while one was open for 6% of the time, Pallas kernels for 4%

profile of v3, /device:TPU:0, one launch (start us, length us, event | category | flops | bytes accessed | tf_op | source)
XLA Modules:
  0.0 275.7 jit_solution(4267626105933664938)
XLA Ops:
  0.6 0.0 copy-start
  0.6 1.3 fusion.24
  1.9 0.7 iota_add_fusion
  2.7 0.1 add.88
  2.7 0.7 iota_compare_fusion.3
  3.5 0.1 lt.32
  3.5 0.0 copy-start.3
  3.6 1.3 copy-done.3
  4.8 13.4 %shard_map.138 = (bf16[3,3,768]{2,1,0:T(4,128)(2,1)S(1)}, bf16[3,32,768]{2,1,0:T(8,128)(2,1)S(1)}, bf16[3,3,768]{2,1,0:T(4,128)(2,1)S(1)}, bf16[24,3,768]{2,1,0:...) custom-call(bf16[24,32,768]{2,1,0:T(8,128)(2,1)S(1)} %bitcast.32, ...), custom_call_target="tpu_custom_call" | custom-call | tf_op jit(solution)/shard_map/pallas_call | solution.py:231
  18.2 0.0 copy-done
  18.3 0.0 copy-start.4
  18.3 4.5 %fusion.11 = bf16[1536,768]{1,0:T(8,128)(2,1)} fusion(bf16[832,768]{1,0:T(8,128)(2,1)S(1)} %copy-done, s32[1536]{0:T(1024)S(1)} %add.88, pred[1536]{0:T(1024)(128)(4,1)S(1)} %lt.32), kind=kOutput, calls=%fused_computation.18 | convolution fusion | flops 1966669824 | bytes 3644928 | tf_op jit(solution)/shard_map/dot_general | solution.py:467
  22.8 0.0 copy-done.4
  22.8 0.0 copy-start.5
  22.8 1.2 maximum_maximum_fusion.padded_ref
  24.0 5.8 %all-to-all-start = ((bf16[32,48,768]{2,1,0:T(8,128)(2,1)}), bf16[32,48,768]{2,1,0:T(8,128)(2,1)}, u32[]{:S(2)}, u32[]{:S(2)}) async-start(bf16[32,48,768]{2,1,0:T(8,128)(2,1)} %bitcast.37), calls=%async_computation | async-start | bytes 4718592 | tf_op jit(solution)/shard_map/all_to_all | solution.py:475
  29.8 0.0 copy-done.5
  29.8 11.2 %shard_map.139 = f32[24,32,768]{2,1,0:T(8,128)S(1)} custom-call(bf16[30,38,768]{2,1,0:T(8,128)(2,1)S(1)} %maximum_maximum_fusion.padded_ref, f32[7,7,768]{2,1,0:T(8,128)S(1)} %copy-done.5), custom_call_target="tpu_custom_call" | custom-call | flops 8580096000 | bytes 41943040 | tf_op jit(solution)/shard_map/pallas_call | solution.py:98
  41.1 0.0 copy-start.1
  41.1 1.4 copy-done.1
  42.5 0.0 copy-start.10
  42.5 1.9 reduce_sum.45
  44.4 0.1 div.15
  44.4 2.0 multiply_reduce_fusion.1
  46.5 0.1 rsqrt.12
  46.6 0.0 copy-done.10
  46.6 1.1 select_reduce_fusion
  47.7 92.5 %all-gather.1 = s32[32,1,1536]{2,1,0:T(1,128)S(1)} all-gather(s32[1,1,1536]{2,1,0:T(1,128)S(1)} %reshape.126), channel_id=2, replica_groups=mesh['scene'=4,'tile'=8] {'scene','tile'}, dimensions={0}, use_global_device_ids=true | all-gather | bytes 202752 | tf_op jit(solution)/shard_map/all_gather | solution.py:479
  140.2 0.1 dynamic-slice_reduce_fusion
  140.4 0.1 eq.34
  140.4 0.0 copy-done.9
  140.4 2.0 multiply_convert_fusion.4
  142.5 0.0 copy-start.7
  142.5 1.0 copy-done.7
  143.5 8.5 %fusion.25 = f32[768,3072]{1,0:T(8,128)} fusion(bf16[768,768]{1,0:T(8,128)(2,1)S(1)} %multiply_convert_fusion.4, bf16[768,3072]{1,0:T(8,128)(2,1)} %param.14), kind=kOutput, calls=%fused_computation.47 | convolution fusion | flops 3623878656 | bytes 15335424 | tf_op jit(solution)/shard_map/dot_general | solution.py:491
  152.0 0.0 all-to-all-done
  152.0 0.0 slice-start
  152.0 4.0 %fusion.10 = f32[768,768]{1,0:T(8,128)S(1)} fusion(bf16[1536,768]{1,0:T(8,128)(2,1)} %bitcast.5, s32[1536]{0:T(1024)S(1)} %eq.34), kind=kOutput, calls=%fused_computation.17 | convolution fusion | flops 1813118976 | bytes 4724736 | tf_op jit(solution)/shard_map/dot_general | solution.py:497
  156.0 0.0 copy-done.11
  156.0 0.0 copy-done.12
  156.0 0.0 copy-start.6
  156.0 0.0 slice-start.1
  156.1 0.0 slice-start.2
  156.1 12.7 %convolution_convert_fusion = bf16[3072,768]{1,0:T(8,128)(2,1)} fusion(f32[768,3072]{1,0:T(8,128)} %fusion.25, f32[3072]{0:T(1024)S(1)} %copy-done.11, f32[768,768]{1,0:T(8,128)S(1)} %fusion.10, f32[768]{0:T(1024)S(1)} %copy-done.12), kind=kOutput, calls=%fused_computation.14 | convolution fusion | flops 3651010560 | bytes 16530432 | tf_op jit(solution)/shard_map/dot_general | solution.py:434
  168.8 0.0 copy-done.6
  168.8 0.0 slice-done
  168.8 0.0 slice-done.1
  168.8 0.0 copy-start.2
  168.8 0.0 slice-start.3
  168.8 10.1 %fusion.6 = bf16[768,3072]{1,0:T(8,128)(2,1)S(1)} fusion(f32[768,3072]{1,0:T(8,128)} %fusion.25, bf16[3072,768]{1,0:T(8,128)(2,1)S(1)} %bitcast.42, f32[3072]{0:T(1024)S(1)} %copy-done.11, f32[768,768]{1,0:T(8,128)S(1)} %fusion.10, f32[768]{0:T(1024)S(1)} %copy-done.12), kind=kOutput, calls=%fused_computation.8 | convolution fusion | flops 3672244224 | bytes 21249024 | tf_op jit(solution)/shard_map/dot_general | solution.py:499
  178.9 0.0 slice-done.2
  178.9 0.0 copy-done.2
  178.9 0.0 slice-done.3
  178.9 0.0 copy-start.8
  179.0 4.3 %multiply_reduce_fusion.2 = (f32[768]{0:T(1024)S(1)}, f32[768]{0:T(1024)S(1)}, f32[768,768]{1,0:T(8,128)S(1)}) fusion(f32[768]{0:T(1024)S(1)} %copy-done.9, f32[768]{0:T(1024)S(1)} %rsqrt.12, f32[768]{0:T(1024)S(1)} %div.15, f32[24,32,768]{2,1,0:T(8,128)S(1)} %copy-done.2, bf16[768,3072]{1,0:T(8,128)(2,1)S(1)} %fusion.6, bf16[768,3072]{1,0:T(8,128)(2,1)S(1)} %bitcast.44), kind=kOutput, calls=%fused_computation.29 | convolution fusion | flops 3627416064 | bytes 14171136 | tf_op jit(solution)/shard_map/dot_general | solution.py:501
  183.2 0.0 copy-done.8
  183.2 5.6 %convolution_convert_fusion.1 = bf16[768,3072]{1,0:T(8,128)(2,1)} fusion(bf16[768,768]{1,0:T(8,128)(2,1)S(1)} %copy-done.8, bf16[768,3072]{1,0:T(8,128)(2,1)S(1)} %fusion.6), kind=kOutput, calls=%fused_computation.15 | convolution fusion | flops 3626237952 | bytes 10616832 | tf_op jit(solution)/shard_map/dot_general | solution.py:434
  188.8 0.9 multiply_convert_fusion.2
  189.7 0.1 fusion.23
  189.8 82.8 %shard_map.140 = (f32[24,3072]{1,0:T(8,128)S(1)}, f32[96,768]{1,0:T(8,128)S(1)}, f32[7,7,768]{2,1,0:T(8,128)S(1)}, bf16[24,32,768]{2,1,0:T(8,128)(2,1)S(1)}) custom-call(bf16[2,2,2,2,2,24,3072]{6,5,4,3,2,1,0:T(8,128)(2,1)} %bitcast.36, bf16[2,2,2,2,2,96,768]{6,5,4,3,2,1,0:T(8,128)(2,1)} %bitcast.35, bf16[24,32,768]{2,1,0:T(8,128)(2,1)S(1)} %bitcast.30, ...), custom_call_target="tpu_custom_call" | custom-call | tf_op jit(solution)/shard_map/pallas_call | solution.py:383
  272.6 1.0 copy.19
  273.6 0.7 copy.20
  274.4 0.7 copy.21
  275.1 0.7 copy.22
  (11 shorter events, 0.0 us)
Async XLA Ops:
  0.6 17.6 %copy-start = (bf16[832,768]{1,0:T(8,128)(2,1)S(1)}, bf16[832,768]{1,0:T(8,128)(2,1)}, u32[]{:S(2)}) copy-start(bf16[832,768]{1,0:T(8,128)(2,1)} %param.18) | copy-start | bytes 3833860
  3.5 1.3 copy-start.3
  18.3 4.5 %copy-start.4 = (bf16[1,1,24,32,768]{4,3,2,1,0:T(8,128)(2,1)S(1)}, bf16[1,1,24,32,768]{4,3,2,1,0:T(8,128)(2,1)}, u32[]{:S(2)}) copy-start(bf16[1,1,24,32,768]{4,3,2,1,0:T(8,128)(2,1)} %param.11) | copy-start | bytes 3538948
  22.8 7.0 %copy-start.5 = (f32[7,7,768]{2,1,0:T(8,128)S(1)}, f32[7,7,768]{2,1,0:T(8,128)}, u32[]{:S(2)}) copy-start(f32[7,7,768]{2,1,0:T(8,128)} %taps_ref.1) | copy-start | bytes 451588
  24.0 128.1 %all-to-all-start = ((bf16[32,48,768]{2,1,0:T(8,128)(2,1)}), bf16[32,48,768]{2,1,0:T(8,128)(2,1)}, u32[]{:S(2)}, u32[]{:S(2)}) async-start(bf16[32,48,768]{2,1,0:T(8,128)(2,1)} %bitcast.37), calls=%async_computation | async-start | bytes 4718592 | tf_op jit(solution)/shard_map/all_to_all | solution.py:475
  41.1 1.4 copy-start.1
  42.5 4.1 %copy-start.10 = (s32[832]{0:T(1024)S(1)}, s32[832]{0:T(1024)}, u32[]{:S(2)}) copy-start(s32[832]{0:T(1024)} %param.19) | copy-start | bytes 9988
  42.5 98.0 %copy-start.9 = (f32[768]{0:T(1024)S(1)}, f32[768]{0:T(1024)}, u32[]{:S(2)}) copy-start(f32[768]{0:T(1024)} %param.13) | copy-start | bytes 9220
  142.5 1.0 copy-start.7
  152.0 4.0 %copy-start.11 = (f32[3072]{0:T(1024)S(1)}, f32[3072]{0:T(1024)}, u32[]{:S(2)}) copy-start(f32[3072]{0:T(1024)} %param.15) | copy-start | bytes 36868
  152.0 4.0 %copy-start.12 = (f32[768]{0:T(1024)S(1)}, f32[768]{0:T(1024)}, u32[]{:S(2)}) copy-start(f32[768]{0:T(1024)} %param.17) | copy-start | bytes 9220
  152.0 16.8 %slice-start = ((s8[4718592]{0:T(1024)(128)(4,1)}), s8[4194304]{0:T(1024)(128)(4,1)S(1)}, s32[]{:S(2)}) async-start(s8[4718592]{0:T(1024)(128)(4,1)} %bitcast.41), calls=%async_computation.1 | async-start | bytes 8388608
  156.0 12.8 %copy-start.6 = (f32[768,768]{1,0:T(8,128)}, f32[768,768]{1,0:T(8,128)S(1)}, u32[]{:S(2)}) copy-start(f32[768,768]{1,0:T(8,128)S(1)} %fusion.10) | copy-start | bytes 7077892
  156.0 12.8 %slice-start.1 = ((s8[4718592]{0:T(1024)(128)(4,1)}), s8[524288]{0:T(1024)(128)(4,1)S(1)}, s32[]{:S(2)}) async-start(s8[4718592]{0:T(1024)(128)(4,1)} %bitcast.41), calls=%async_computation.2 | async-start | bytes 1048576
  156.1 22.9 %slice-start.2 = ((s8[4718592]{0:T(1024)(128)(4,1)}), s8[4194304]{0:T(1024)(128)(4,1)S(1)}, s32[]{:S(2)}) async-start(s8[4718592]{0:T(1024)(128)(4,1)} %bitcast.43), calls=%async_computation.3 | async-start | bytes 8388608
  168.8 10.1 %copy-start.2 = (f32[24,32,768]{2,1,0:T(8,128)S(1)}, f32[24,32,768]{2,1,0:T(8,128)}, u32[]{:S(2)}) copy-start(f32[24,32,768]{2,1,0:T(8,128)} %copy-done.1) | copy-start | bytes 7077892
  168.8 10.1 %slice-start.3 = ((s8[4718592]{0:T(1024)(128)(4,1)}), s8[524288]{0:T(1024)(128)(4,1)S(1)}, s32[]{:S(2)}) async-start(s8[4718592]{0:T(1024)(128)(4,1)} %bitcast.43), calls=%async_computation.4 | async-start | bytes 1048576
  178.9 4.3 %copy-start.8 = (bf16[768,768]{1,0:T(8,128)(2,1)S(1)}, bf16[768,768]{1,0:T(8,128)(2,1)}, u32[]{:S(2)}) copy-start(bf16[768,768]{1,0:T(8,128)(2,1)} %copy-done.7) | copy-start | bytes 3538948
